TPU v7x, 32 devices: a whole 2x2x4 slice. The times are simulated.
32 devices in a mesh: row: 8 (over z, core), col: 4 (over y, x).
Axes of the slice: x: 2, y: 2, z: 4, core: 2. Of those that a mesh axis runs over, the one named last changes fastest.
Arguments:
- inv_diag: bfloat16 [4, 8192, 8192], P(None, 'col', 'row'), as said below
- off_diag: bfloat16 [4, 1792, 8192], P(None, 'row', 'col'), may hold values from -0.0625 to 0.0625
- rhs: bfloat16 [4, 8192, 768], P(None, 'row'), may hold values from -6 to 6
- anc_rhs: float32 [1792, 768], P('row'), may hold values from -12 to 12
- dest_device: int32 [56, 4, 1], replicated, may hold values from 0 to 7, as said below
- dest_slot: int32 [56, 4], replicated, may hold values from 0 to 6
Outputs:
- solution: bfloat16 [4, 8192, 768], P(None, ('col', 'row'))
- anc_out: float32 [1792, 768], P('row')
Inputs may be any that keep to these rules, and one draw needn't show every extreme that they name: inv_diag[s] is zero above its diagonal. Within one supernode s, distinct row blocks j belong to distinct ancestor blocks. Among the 28 entries dest_device[j, s] with j in one index of row's range of 7 blocks, every value occurs either 0 or exactly 7 times.
All inputs are finite; a program needn't handle non-finite values.
Results may differ from a plain program's by a relative error of at most 0.014.
Values may be sent and summed in bfloat16 or wider, within the bound.
No kernel may reach another device: no remote copies, remote signals or barrier semaphores. Data moves between devices by JAX's collectives and lax.ppermute only.
A program may use at most 128 MiB of HBM per device.

v0:
```python
import functools

import jax
import jax.numpy as jnp
from jax import lax
from jax.experimental import pallas as pl
from jax.experimental.pallas import tpu as pltpu
from jax.sharding import PartitionSpec as P

SNODES = 4
BLOCK = 32
HALVES = 2
STREAMS = 2
F32 = jnp.float32
BF16 = jnp.bfloat16


def add16(*terms):
    return functools.reduce(lambda a, b: a + b, [t.astype(F32) for t in terms]).astype(BF16)


def pick(array, index, axis):
    return lax.dynamic_index_in_dim(array, index, axis, keepdims=False)


def after(value, *earlier):
    return lax.optimization_barrier((value,) + earlier)[0]


def update_kernel(table_ref, place_ref, off_ref, *refs):
    pieces, out_ref, total = refs[:-2], refs[-2], refs[-1]
    nz = off_ref.shape[1]
    z, core = place_ref[0], place_ref[1]
    step = 2 * core - 1
    blocks = off_ref.shape[3] // BLOCK
    per = SNODES // STREAMS
    total[...] = jnp.zeros_like(total)
    for s in range(SNODES):
        own = pieces[(s // per) * nz]
        part = jnp.dot(off_ref[s, z, core], own[s % per, core], preferred_element_type=F32)
        for t in range(1, nz):
            piece = pieces[(s // per) * nz + t]
            chip = jnp.clip(z + step * t, 0, nz - 1)
            for q in range(2):
                part += jnp.dot(off_ref[s, chip, q], piece[s % per, q], preferred_element_type=F32)
        for b in range(blocks):
            total[table_ref[s * blocks + b]] += part[b * BLOCK : (b + 1) * BLOCK]
    out_ref[...] = total[...].astype(out_ref.dtype)


def apply_update(table, place, off, pieces, anc_blocks):
    width = pieces[0].shape[-1]
    flops = 2 * off.size * width
    return pl.pallas_call(
        update_kernel,
        out_shape=jax.ShapeDtypeStruct((anc_blocks, BLOCK, width), BF16),
        in_specs=[pl.BlockSpec(memory_space=pltpu.SMEM)] * 2
        + [pl.BlockSpec(memory_space=pltpu.VMEM)] * (1 + len(pieces)),
        out_specs=pl.BlockSpec(memory_space=pltpu.VMEM),
        scratch_shapes=[pltpu.VMEM((anc_blocks, BLOCK, width), F32)],
        compiler_params=pltpu.CompilerParams(vmem_limit_bytes=48 * 1024 * 1024),
        cost_estimate=pl.CostEstimate(
            flops=flops, bytes_accessed=off.size * 2 + anc_blocks * BLOCK * width * 2, transcendentals=0
        ),
    )(table, place, off, *pieces)


def per_device(inv_diag, off_diag, rhs, anc_rhs, dest_device, dest_slot):
    n_row, n_col = lax.axis_size("row"), lax.axis_size("col")
    nz = n_row // 2
    row, col = lax.axis_index("row"), lax.axis_index("col")
    z, core = row // 2, row % 2
    side = 1 - 2 * core
    own_rows = inv_diag.shape[1] // n_row
    anc_dev = anc_rhs.shape[0] // BLOCK
    anc_blocks = n_row * anc_dev
    width = rhs.shape[2] // HALVES
    per = SNODES // STREAMS
    pair = [(r, r ^ 1) for r in range(n_row)]

    def hop(value, sources):
        up = [(2 * i, 2 * i + 2) for i in sources if i + 1 < nz]
        down = [(2 * (nz - 1 - i) + 1, 2 * (nz - 2 - i) + 1) for i in sources if i + 1 < nz]
        return lax.ppermute(value, "row", up + down)

    def product(s, n, *earlier):
        part = after(rhs[s * per : (s + 1) * per, :, n * width : (n + 1) * width], *earlier)
        terms = jnp.einsum(
            "swk,skn->swn", inv_diag[s * per : (s + 1) * per], part, preferred_element_type=F32
        ).astype(BF16)
        return terms.reshape(per, nz, 2, own_rows, width)

    def sum_cores(terms):
        away = jnp.stack([pick(terms, (z - side * j) % nz, 1) for j in range(1, nz)])
        other = lax.ppermute(away, "row", pair)
        return [pick(terms, z, 1)] + [
            add16(pick(terms, (z + side * j) % nz, 1), other[j - 1]) for j in range(1, nz)
        ]

    def share(total):
        total = total.reshape(nz, 2, anc_dev, n_col, BLOCK // n_col, width)
        total = add16(pick(total, core, 1), lax.ppermute(pick(total, 1 - core, 1), "row", pair))
        turns = [[(i, i ^ d) for i in range(n_col)] for d in range(1, n_col)]
        total = add16(
            pick(total, col, 2),
            *[lax.ppermute(pick(total, col ^ d, 2), "col", turns[d - 1]) for d in range(1, n_col)],
        )
        moves = [
            [(2 * i + q, 2 * ((i + d) % nz) + q) for i in range(nz) for q in range(2)] for d in range(1, nz)
        ]
        total = add16(
            pick(total, z, 0),
            *[lax.ppermute(pick(total, (z + d) % nz, 0), "row", moves[d - 1]) for d in range(1, nz)],
        )
        whole = jnp.zeros((anc_dev, n_col) + total.shape[1:], BF16)
        whole = lax.dynamic_update_index_in_dim(whole, total, col, 1)
        for d in range(1, n_col):
            other = lax.ppermute(total, "col", turns[d - 1])
            whole = lax.dynamic_update_index_in_dim(whole, other, col ^ d, 1)
        return whole.reshape(anc_dev * BLOCK, width)

    per_dev = off_diag.shape[1] // BLOCK
    target = (dest_device[:, :, 0] * anc_dev + dest_slot).reshape(n_row, per_dev, SNODES)
    table = jnp.concatenate([pick(target, row, 0), pick(target, row ^ 1, 0)], axis=0).T.reshape(-1)
    place = jnp.stack([z, core]).astype(jnp.int32)

    terms = [[None] * HALVES for _ in range(STREAMS)]
    last = ()
    for s in range(STREAMS):
        terms[s][0] = product(s, 0, *last)
        last = (terms[s][0],)
        terms[s][0] = sum_cores(terms[s][0])

    own = [[None] * HALVES for _ in range(STREAMS)]
    pieces = [[None] * HALVES for _ in range(STREAMS)]
    totals = []
    for s in range(STREAMS):
        flow = ()
        for t in range(1, nz):
            flow = (hop(add16(terms[s][0][nz - t], *flow), range(t)),)
            if t == 1:
                for n in range(1, HALVES):
                    terms[s][n] = sum_cores(product(s, n, flow[0]))
        for n in range(HALVES):
            mine = add16(terms[s][n][0], *flow)
            flow = ()
            own[s][n] = add16(mine, lax.ppermute(mine, "row", pair))
            got = [own[s][n]]
            for t in range(1, nz + 1):
                if t < nz:
                    got.append(hop(got[-1], range(t - 1, nz)))
                if t > 1 and n + 1 < HALVES:
                    send = add16(terms[s][n + 1][nz - t + 1], *flow)
                    if t == 2:
                        send = after(send, got[1])
                    flow = (hop(send, range(t - 1)),)
            pieces[s][n] = got
    off = off_diag.reshape(SNODES, off_diag.shape[1], nz, 2, own_rows).transpose(0, 2, 3, 1, 4)
    off = jnp.concatenate([off, lax.ppermute(after(off, terms[0][1][0]), "row", pair)], axis=3)
    for n in range(HALVES):
        flat = [p for s in range(STREAMS) for p in pieces[s][n]]
        totals.append(share(apply_update(table, place, off, flat, anc_blocks)))
    solution = jnp.concatenate(
        [jnp.concatenate([pick(own[s][n], core, 1) for n in range(HALVES)], axis=2) for s in range(STREAMS)],
        axis=0,
    )
    anc_out = anc_rhs - jnp.concatenate(totals, axis=1).astype(F32)
    return (solution, anc_out)


def solution(mesh):
    in_specs = (
        P(None, "col", "row"),
        P(None, "row", "col"),
        P(None, "row", None),
        P("row", None),
        P(),
        P(),
    )
    out_specs = (P(None, ("col", "row"), None), P("row", None))
    return jax.shard_map(
        per_device, mesh=mesh, in_specs=in_specs, out_specs=out_specs, check_vma=False
    )
```

profile of v0, /device:TPU:0, one launch (start us, length us, event | category | flops | bytes accessed | tf_op | source)
XLA Modules:
  0.0 346.5 jit_solution(8570041506791365341)
XLA Ops:
  0.7 5.2 %fusion.55 = (bf16[2,1024,384]{2,1,0:T(8,128)(2,1)}, bf16[2,1024,384]{2,1,0:T(8,128)(2,1)S(1)}, bf16[2,1024,384]{2,1,0:T(8,128)(2,1)}, bf16[2,1024,384]{2,1,0:T(8,128)(2,1)S(1)}) fusion(bf16[4,1024,768]{2,1,0:T(8,128)(2,1)} %param.8), kind=kLoop, calls=%fused_computation.140 | loop fusion | bytes 12582912 | tf_op jit(solution)/shard_map/slice | solution.py:87
  5.9 9.6 %convolution_convert_fusion = bf16[2,2048,384]{2,1,0:T(8,128)(2,1)} fusion(bf16[4,2048,1024]{2,1,0:T(8,128)(2,1)} %param.6, bf16[2,1024,384]{2,1,0:T(8,128)(2,1)S(1)} %get-tuple-element.21), kind=kOutput, calls=%fused_computation.11 | convolution fusion | flops 3222798336 | bytes 21495808 | tf_op jit(solution)/shard_map/swk,skn->swn/dot_general | solution.py:88
  15.5 8.8 %fusion.21 = bf16[2,2048,384]{1,2,0:T(8,128)(2,1)} fusion(bf16[2,1024,384]{2,1,0:T(8,128)(2,1)S(1)} %get-tuple-element.10, bf16[4,2048,1024]{2,1,0:T(8,128)(2,1)} %param.6), kind=kOutput, calls=%fused_computation.14 | convolution fusion | flops 3222798336 | bytes 13107200 | tf_op jit(solution)/shard_map/swk,skn->swn/dot_general | solution.py:88
  24.2 3.4 copy.32
  28.0 1.8 pad_maximum_fusion.3
  31.8 1.7 pad_maximum_fusion.1
  34.7 2.2 fusion.28
  36.9 5.7 %collective-permute-start.12 = (bf16[2,2,256,384]{3,2,1,0:T(8,128)(2,1)}, bf16[2,2,256,384]{3,2,1,0:T(8,128)(2,1)}, u32[]{:S(2)}, u32[]{:S(2)}) collective-permute-start(bf16[2,2,256,384]{3,2,1,0:T(8,128)(2,1)} %fusion.28), channel_id=1, source_target_pairs={{0,8},{28,20},{1,9},{29,21},{2,10},{30,22},{3,11},{31,23}} | collective-permute-start | bytes 2359304 | tf_op jit(solution)/shard_map/ppermute | solution.py:84
  42.7 1.7 fusion.35
  44.4 1.6 collective-permute-start.1
  46.0 5.6 %collective-permute-done.12 = bf16[2,2,256,384]{3,2,1,0:T(8,128)(2,1)} collective-permute-done((bf16[2,2,256,384]{3,2,1,0:T(8,128)(2,1)}, bf16[2,2,256,384]{3,2,1,0:T(8,128)(2,1)}, u32[]{:S(2)}, u32[]{:S(2)}) %collective-permute-start.12) | collective-permute-done | bytes 786464 | tf_op jit(solution)/shard_map/ppermute | solution.py:84
  51.6 8.7 %fusion.18 = bf16[2,2048,384]{1,2,0:T(8,128)(2,1)} fusion(bf16[2,1024,384]{2,1,0:T(8,128)(2,1)S(1)} %copy-done.14, bf16[4,2048,1024]{2,1,0:T(8,128)(2,1)} %param.6), kind=kOutput, calls=%fused_computation.13 | convolution fusion | flops 3222798336 | bytes 13107200 | tf_op jit(solution)/shard_map/swk,skn->swn/dot_general | solution.py:88
  60.3 2.6 add_convert_fusion.5
  62.9 5.4 %collective-permute-start.13 = (bf16[2,2,256,384]{3,2,1,0:T(8,128)(2,1)}, bf16[2,2,256,384]{3,2,1,0:T(8,128)(2,1)}, u32[]{:S(2)}, u32[]{:S(2)}) collective-permute-start(bf16[2,2,256,384]{3,2,1,0:T(8,128)(2,1)} %add_convert_fusion.5), channel_id=1, source_target_pairs={{0,8},{8,16},{28,20},{20,12},{1,9},{9,17},{29,21},{21,13},{2,10},{... | collective-permute-start | bytes 2359304 | tf_op jit(solution)/shard_map/ppermute | solution.py:84
  68.3 2.6 add_convert_fusion.12
  70.9 2.2 collective-permute-start.2
  73.1 8.7 %fusion.15 = bf16[2,2048,384]{1,2,0:T(8,128)(2,1)} fusion(bf16[2,1024,384]{2,1,0:T(8,128)(2,1)S(1)} %copy-done.13, bf16[4,2048,1024]{2,1,0:T(8,128)(2,1)} %param.6), kind=kOutput, calls=%fused_computation.12 | convolution fusion | flops 3222798336 | bytes 13107200 | tf_op jit(solution)/shard_map/swk,skn->swn/dot_general | solution.py:88
  81.8 3.4 copy.38
  85.2 5.4 %copy.27 = bf16[2,2048,384]{2,1,0:T(8,128)(2,1)} copy(bf16[2,2048,384]{1,2,0:T(8,128)(2,1)} %fusion.15) | data formatting | bytes 6291456 | tf_op jit(solution)/shard_map/convert_element_type | solution.py:90
  90.6 3.0 add_convert_fusion.11
  93.6 2.2 collective-permute-start.3
  95.8 1.8 dynamic-slice_bitcast_fusion.2
  97.6 1.7 pad_maximum_fusion.2
  100.3 2.6 add_convert_fusion.4
  102.9 2.2 collective-permute-start.14
  105.1 1.9 pad_maximum_fusion.4
  109.2 4.8 %collective-permute-done.14 = bf16[2,2,256,384]{3,2,1,0:T(8,128)(2,1)} collective-permute-done((bf16[2,2,256,384]{3,2,1,0:T(8,128)(2,1)}, bf16[2,2,256,384]{3,2,1,0:T(8,128)(2,1)}, u32[]{:S(2)}, u32[]{:S(2)}) %collective-permute-start.14) | collective-permute-done | bytes 786464 | tf_op jit(solution)/shard_map/ppermute | solution.py:84
  117.0 15.3 %collective-permute-start.6 = (bf16[2,2,256,384]{3,2,1,0:T(8,128)(2,1)S(1)}, bf16[2,2,256,384]{3,2,1,0:T(8,128)(2,1)S(1)}, u32[]{:S(2)}, u32[]{:S(2)}) collective-permute-start(bf16[2,2,256,384]{3,2,1,0:T(8,128)(2,1)S(1)} %add_convert_fusion.10.refs_0_), channel_id=1, source_target_pairs={{0,8},{8,16},{16,24},{28,20},{20,12},{12,4},{1,9},{9,17},{17,25},{... | collective-permute-start | bytes 2359304 | tf_op jit(solution)/shard_map/ppermute | solution.py:84
  132.6 2.1 collective-permute-start.17
  136.1 5.8 %collective-permute-done.6.refs_1_ = bf16[2,2,256,384]{3,2,1,0:T(8,128)(2,1)S(1)} collective-permute-done((bf16[2,2,256,384]{3,2,1,0:T(8,128)(2,1)S(1)}, bf16[2,2,256,384]{3,2,1,0:T(8,128)(2,1)S(1)}, u32[]{:S(2)}, u32[]{:S(2)}) %collective-permute-start.6) | collective-permute-done | bytes 786464 | tf_op jit(solution)/shard_map/ppermute | solution.py:84
  141.8 4.4 %collective-permute-start.7 = (bf16[2,2,256,384]{3,2,1,0:T(8,128)(2,1)S(1)}, bf16[2,2,256,384]{3,2,1,0:T(8,128)(2,1)S(1)}, u32[]{:S(2)}, u32[]{:S(2)}) collective-permute-start(bf16[2,2,256,384]{3,2,1,0:T(8,128)(2,1)S(1)} %fusion.32), channel_id=1, source_target_pairs={{0,8},{28,20},{1,9},{29,21},{2,10},{30,22},{3,11},{31,23}} | collective-permute-start | bytes 2359304 | tf_op jit(solution)/shard_map/ppermute | solution.py:84
  146.5 3.8 %collective-permute-done.17.refs_5_ = bf16[2,2,256,384]{3,2,1,0:T(8,128)(2,1)S(1)} collective-permute-done((bf16[2,2,256,384]{3,2,1,0:T(8,128)(2,1)S(1)}, bf16[2,2,256,384]{3,2,1,0:T(8,128)(2,1)S(1)}, u32[]{:S(2)}, u32[]{:S(2)}) %collective-permute-start.17) | collective-permute-done | bytes 786464 | tf_op jit(solution)/shard_map/ppermute | solution.py:84
  150.3 4.4 %collective-permute-start.18 = (bf16[2,2,256,384]{3,2,1,0:T(8,128)(2,1)S(1)}, bf16[2,2,256,384]{3,2,1,0:T(8,128)(2,1)S(1)}, u32[]{:S(2)}, u32[]{:S(2)}) collective-permute-start(bf16[2,2,256,384]{3,2,1,0:T(8,128)(2,1)S(1)} %fusion.24), channel_id=1, source_target_pairs={{0,8},{28,20},{1,9},{29,21},{2,10},{30,22},{3,11},{31,23}} | collective-permute-start | bytes 2359304 | tf_op jit(solution)/shard_map/ppermute | solution.py:84
  154.7 4.0 %collective-permute-done.7 = bf16[2,2,256,384]{3,2,1,0:T(8,128)(2,1)S(1)} collective-permute-done((bf16[2,2,256,384]{3,2,1,0:T(8,128)(2,1)S(1)}, bf16[2,2,256,384]{3,2,1,0:T(8,128)(2,1)S(1)}, u32[]{:S(2)}, u32[]{:S(2)}) %collective-permute-start.7) | collective-permute-done | bytes 786464 | tf_op jit(solution)/shard_map/ppermute | solution.py:84
  160.1 4.4 %collective-permute-start.8 = (bf16[2,2,256,384]{3,2,1,0:T(8,128)(2,1)S(1)}, bf16[2,2,256,384]{3,2,1,0:T(8,128)(2,1)S(1)}, u32[]{:S(2)}, u32[]{:S(2)}) collective-permute-start(bf16[2,2,256,384]{3,2,1,0:T(8,128)(2,1)S(1)} %add_convert_fusion.9), channel_id=1, source_target_pairs={{0,8},{8,16},{28,20},{20,12},{1,9},{9,17},{29,21},{21,13},{2,10},{... | collective-permute-start | bytes 2359304 | tf_op jit(solution)/shard_map/ppermute | solution.py:84
  164.6 2.5 collective-permute-done.18
  167.4 4.4 %collective-permute-start.19 = (bf16[2,2,256,384]{3,2,1,0:T(8,128)(2,1)S(1)}, bf16[2,2,256,384]{3,2,1,0:T(8,128)(2,1)S(1)}, u32[]{:S(2)}, u32[]{:S(2)}) collective-permute-start(bf16[2,2,256,384]{3,2,1,0:T(8,128)(2,1)S(1)} %add_convert_fusion.2), channel_id=1, source_target_pairs={{0,8},{8,16},{28,20},{20,12},{1,9},{9,17},{29,21},{21,13},{2,10},{... | collective-permute-start | bytes 2359304 | tf_op jit(solution)/shard_map/ppermute | solution.py:84
  171.9 3.7 %collective-permute-done.8 = bf16[2,2,256,384]{3,2,1,0:T(8,128)(2,1)S(1)} collective-permute-done((bf16[2,2,256,384]{3,2,1,0:T(8,128)(2,1)S(1)}, bf16[2,2,256,384]{3,2,1,0:T(8,128)(2,1)S(1)}, u32[]{:S(2)}, u32[]{:S(2)}) %collective-permute-start.8) | collective-permute-done | bytes 786464 | tf_op jit(solution)/shard_map/ppermute | solution.py:84
  175.5 2.3 add_convert_fusion.8
  177.9 4.4 %collective-permute-start.9 = (bf16[2,2,256,384]{3,2,1,0:T(8,128)(2,1)}, bf16[2,2,256,384]{3,2,1,0:T(8,128)(2,1)S(1)}, u32[]{:S(2)}, u32[]{:S(2)}) collective-permute-start(bf16[2,2,256,384]{3,2,1,0:T(8,128)(2,1)} %add_convert_fusion.8), channel_id=1, source_target_pairs={{0,8},{8,16},{16,24},{28,20},{20,12},{12,4},{1,9},{9,17},{17,25},{... | collective-permute-start | bytes 2359304 | tf_op jit(solution)/shard_map/ppermute | solution.py:84
  182.3 1.7 collective-permute-done.19
  185.2 4.4 %collective-permute-start.20 = (bf16[2,2,256,384]{3,2,1,0:T(8,128)(2,1)}, bf16[2,2,256,384]{3,2,1,0:T(8,128)(2,1)S(1)}, u32[]{:S(2)}, u32[]{:S(2)}) collective-permute-start(bf16[2,2,256,384]{3,2,1,0:T(8,128)(2,1)} %add_convert_fusion.1), channel_id=1, source_target_pairs={{0,8},{8,16},{16,24},{28,20},{20,12},{12,4},{1,9},{9,17},{17,25},{... | collective-permute-start | bytes 2359304 | tf_op jit(solution)/shard_map/ppermute | solution.py:84
  189.6 7.1 %reshape.123 = bf16[4,224,4,2,256]{4,3,2,1,0:T(2,128)(2,1)} reshape(bf16[4,224,2048]{2,1,0:T(8,128)(2,1)} %param.7) | data formatting | bytes 7340032 | tf_op jit(solution)/shard_map/reshape | solution.py:158
  196.8 4.9 %copy.72 = bf16[4,224,4,2,256]{4,1,3,2,0:T(8,128)(2,1)} copy(bf16[4,224,4,2,256]{4,3,2,1,0:T(2,128)(2,1)} %reshape.123) | data formatting | bytes 7340032 | tf_op jit(solution)/shard_map/reshape | solution.py:158
  205.0 5.2 %collective-permute-done.10 = bf16[2,2,256,384]{3,2,1,0:T(8,128)(2,1)S(1)} collective-permute-done((bf16[2,2,256,384]{3,2,1,0:T(8,128)(2,1)S(1)}, bf16[2,2,256,384]{3,2,1,0:T(8,128)(2,1)S(1)}, u32[]{:S(2)}, u32[]{:S(2)}) %collective-permute-start.10) | collective-permute-done | bytes 786464 | tf_op jit(solution)/shard_map/ppermute | solution.py:147
  210.4 2.8 collective-permute-start.37
  213.4 2.3 collective-permute-start.40
  215.7 6.1 %collective-permute-done.37.refs_1_ = bf16[2,2,256,384]{3,2,1,0:T(8,128)(2,1)} collective-permute-done((bf16[2,2,256,384]{3,2,1,0:T(8,128)(2,1)S(1)}, bf16[2,2,256,384]{3,2,1,0:T(8,128)(2,1)}, u32[]{:S(2)}, u32[]{:S(2)}) %collective-permute-start.37) | collective-permute-done | bytes 786464 | tf_op jit(solution)/shard_map/ppermute | solution.py:84
  223.3 6.9 %collective-permute-done.40.refs_5_ = bf16[2,2,256,384]{3,2,1,0:T(8,128)(2,1)} collective-permute-done((bf16[2,2,256,384]{3,2,1,0:T(8,128)(2,1)S(1)}, bf16[2,2,256,384]{3,2,1,0:T(8,128)(2,1)}, u32[]{:S(2)}, u32[]{:S(2)}) %collective-permute-start.40) | collective-permute-done | bytes 786464 | tf_op jit(solution)/shard_map/ppermute | solution.py:84
  230.2 1.6 collective-permute-start.41
  236.6 1.6 collective-permute-start.42
  241.5 6.7 %pad_maximum_fusion.off_ref = bf16[4,4,2,448,256]{4,3,2,1,0:T(8,128)(2,1)} fusion(bf16[4,4,2,224,256]{4,3,2,1,0:T(8,128)(2,1)} %collective-permute-done.22, bf16[4,4,2,224,256]{4,3,2,1,0:T(8,128)(2,1)} %bitcast.282), kind=kLoop, calls=%fused_computation.6 | loop fusion | flops 14680064 | bytes 14680064 | tf_op jit(solution)/shard_map/concatenate | solution.py:159
  248.3 9.5 %shard_map.78 = bf16[56,32,384]{2,1,0:T(8,128)(2,1)} custom-call(s32[56]{0:T(128)S(1)} %reshape.122.table_ref, s32[2]{0:T(128)S(1)} %pad_add_fusion.place_ref, bf16[4,4,2,448,256]{4,3,2,1,0:T(8,128)(2,1)} %pad_maximum_fusion.off_ref, bf16[2,2,256,384]{3,2,1,0:T(8,128)(2,1)S(1)} %add_convert_fusion.6.refs_0_, ...), custom_call_target="tpu_custom_call" | custom-call | flops 2818572288 | bytes 8716288 | tf_op jit(solution)/shard_map/pallas_call | solution.py:54
  259.0 34.4 %collective-permute-start.43 = (bf16[4,7,4,8,384]{4,3,2,1,0:T(8,128)(2,1)S(1)}, bf16[4,7,4,8,384]{4,3,2,1,0:T(8,128)(2,1)S(1)}, u32[]{:S(2)}, u32[]{:S(2)}) collective-permute-start(bf16[4,7,4,8,384]{4,3,2,1,0:T(8,128)(2,1)S(1)} %dynamic-slice_bitcast_fusion.13), channel_id=1, source_target_pairs={{0,4},{4,0},{8,12},{12,8},{16,20},{20,16},{24,28},{28,24},{1,5},{5... | collective-permute-start | bytes 2064392 | tf_op jit(solution)/shard_map/ppermute | solution.py:102
  293.5 8.7 %shard_map.77 = bf16[56,32,384]{2,1,0:T(8,128)(2,1)} custom-call(s32[56]{0:T(128)S(1)} %reshape.122.table_ref, s32[2]{0:T(128)S(1)} %pad_add_fusion.place_ref, bf16[4,4,2,448,256]{4,3,2,1,0:T(8,128)(2,1)} %pad_maximum_fusion.off_ref, bf16[2,2,256,384]{3,2,1,0:T(8,128)(2,1)S(1)} %add_convert_fusion.10.refs_0_, bf16[2,2,256,384]{3,2,1,0:T(8,128)(2,1)S(1)} %copy-done.1, ...), custom_call_target="tpu_custom_call" | custom-call | flops 2818572288 | bytes 8716288 | tf_op jit(solution)/shard_map/pallas_call | solution.py:54
  303.4 6.1 %collective-permute-start.27 = (bf16[4,7,4,8,384]{4,3,2,1,0:T(8,128)(2,1)S(1)}, bf16[4,7,4,8,384]{4,3,2,1,0:T(8,128)(2,1)S(1)}, u32[]{:S(2)}, u32[]{:S(2)}) collective-permute-start(bf16[4,7,4,8,384]{4,3,2,1,0:T(8,128)(2,1)S(1)} %dynamic-slice_bitcast_fusion.14), channel_id=1, source_target_pairs={{0,4},{4,0},{8,12},{12,8},{16,20},{20,16},{24,28},{28,24},{1,5},{5... | collective-permute-start | bytes 2064392 | tf_op jit(solution)/shard_map/ppermute | solution.py:102
  311.7 2.5 collective-permute-start.46
  315.6 2.5 collective-permute-start.30
  321.5 2.3 collective-permute-done.45
  325.2 2.1 collective-permute-done.30
  327.4 2.7 collective-permute-done.29
  333.3 1.6 collective-permute-start.50
  334.9 1.6 collective-permute-start.51
  343.2 2.1 collective-permute-done.36
  (152 shorter events, 49.6 us)
Async XLA Ops:
  27.6 32.7 %copy-start.8 = (bf16[2,2048,384]{2,1,0:T(8,128)(2,1)}, bf16[2,2048,384]{2,1,0:T(8,128)(2,1)S(1)}, u32[]{:S(2)}) copy-start(bf16[2,2048,384]{2,1,0:T(8,128)(2,1)S(1)} %copy.32) | copy-start | bytes 9437188
  29.7 5.0 %collective-permute-start.11 = (bf16[3,2,2,256,384]{4,3,2,1,0:T(8,128)(2,1)}, bf16[3,2,2,256,384]{4,3,2,1,0:T(8,128)(2,1)}, u32[]{:S(2)}, u32[]{:S(2)}) collective-permute-start(bf16[3,2,2,256,384]{4,3,2,1,0:T(8,128)(2,1)} %pad_maximum_fusion.3), channel_id=1, source_target_pairs={{0,4},{4,0},{8,12},{12,8},{16,20},{20,16},{24,28},{28,24},{1,5},{5... | collective-permute-start | bytes 7077896 | tf_op jit(solution)/shard_map/ppermute | solution.py:95
  33.5 9.2 %collective-permute-start = (bf16[3,2,2,256,384]{4,3,2,1,0:T(8,128)(2,1)}, bf16[3,2,2,256,384]{4,3,2,1,0:T(8,128)(2,1)}, u32[]{:S(2)}, u32[]{:S(2)}) collective-permute-start(bf16[3,2,2,256,384]{4,3,2,1,0:T(8,128)(2,1)} %pad_maximum_fusion.1), channel_id=1, source_target_pairs={{0,4},{4,0},{8,12},{12,8},{16,20},{20,16},{24,28},{28,24},{1,5},{5... | collective-permute-start | bytes 7077896 | tf_op jit(solution)/shard_map/ppermute | solution.py:95
  36.9 14.7 %collective-permute-start.12 = (bf16[2,2,256,384]{3,2,1,0:T(8,128)(2,1)}, bf16[2,2,256,384]{3,2,1,0:T(8,128)(2,1)}, u32[]{:S(2)}, u32[]{:S(2)}) collective-permute-start(bf16[2,2,256,384]{3,2,1,0:T(8,128)(2,1)} %fusion.28), channel_id=1, source_target_pairs={{0,8},{28,20},{1,9},{29,21},{2,10},{30,22},{3,11},{31,23}} | collective-permute-start | bytes 2359304 | tf_op jit(solution)/shard_map/ppermute | solution.py:84
  42.7 8.9 %copy-start.14 = (bf16[2,1024,384]{2,1,0:T(8,128)(2,1)S(1)}, bf16[2,1024,384]{2,1,0:T(8,128)(2,1)}, u32[]{:S(2)}) copy-start(bf16[2,1024,384]{2,1,0:T(8,128)(2,1)} %get-tuple-element.11) | copy-start | bytes 4718596
  44.4 16.0 %collective-permute-start.1 = (bf16[2,2,256,384]{3,2,1,0:T(8,128)(2,1)S(1)}, bf16[2,2,256,384]{3,2,1,0:T(8,128)(2,1)S(1)}, u32[]{:S(2)}, u32[]{:S(2)}) collective-permute-start(bf16[2,2,256,384]{3,2,1,0:T(8,128)(2,1)S(1)} %fusion.35), channel_id=1, source_target_pairs={{0,8},{28,20},{1,9},{29,21},{2,10},{30,22},{3,11},{31,23}} | collective-permute-start | bytes 2359304 | tf_op jit(solution)/shard_map/ppermute | solution.py:84
  62.9 10.2 %copy-start.13 = (bf16[2,1024,384]{2,1,0:T(8,128)(2,1)S(1)}, bf16[2,1024,384]{2,1,0:T(8,128)(2,1)}, u32[]{:S(2)}) copy-start(bf16[2,1024,384]{2,1,0:T(8,128)(2,1)} %get-tuple-element.8) | copy-start | bytes 4718596
  62.9 36.4 %collective-permute-start.13 = (bf16[2,2,256,384]{3,2,1,0:T(8,128)(2,1)}, bf16[2,2,256,384]{3,2,1,0:T(8,128)(2,1)}, u32[]{:S(2)}, u32[]{:S(2)}) collective-permute-start(bf16[2,2,256,384]{3,2,1,0:T(8,128)(2,1)} %add_convert_fusion.5), channel_id=1, source_target_pairs={{0,8},{8,16},{28,20},{20,12},{1,9},{9,17},{29,21},{21,13},{2,10},{... | collective-permute-start | bytes 2359304 | tf_op jit(solution)/shard_map/ppermute | solution.py:84
  70.9 19.7 %collective-permute-start.2 = (bf16[2,2,256,384]{3,2,1,0:T(8,128)(2,1)}, bf16[2,2,256,384]{3,2,1,0:T(8,128)(2,1)}, u32[]{:S(2)}, u32[]{:S(2)}) collective-permute-start(bf16[2,2,256,384]{3,2,1,0:T(8,128)(2,1)} %add_convert_fusion.12), channel_id=1, source_target_pairs={{0,8},{8,16},{28,20},{20,12},{1,9},{9,17},{29,21},{21,13},{2,10},{... | collective-permute-start | bytes 2359304 | tf_op jit(solution)/shard_map/ppermute | solution.py:84
  85.2 10.6 %copy-start.4 = (bf16[2,2048,384]{2,1,0:T(8,128)(2,1)}, bf16[2,2048,384]{2,1,0:T(8,128)(2,1)S(1)}, u32[]{:S(2)}) copy-start(bf16[2,2048,384]{2,1,0:T(8,128)(2,1)S(1)} %copy.38) | copy-start | bytes 9437188
  93.6 13.5 %collective-permute-start.3 = (bf16[2,2,256,384]{3,2,1,0:T(8,128)(2,1)}, bf16[2,2,256,384]{3,2,1,0:T(8,128)(2,1)}, u32[]{:S(2)}, u32[]{:S(2)}) collective-permute-start(bf16[2,2,256,384]{3,2,1,0:T(8,128)(2,1)} %add_convert_fusion.11), channel_id=1, source_target_pairs={{0,8},{8,16},{16,24},{28,20},{20,12},{12,4},{1,9},{9,17},{17,25},{... | collective-permute-start | bytes 2359304 | tf_op jit(solution)/shard_map/ppermute | solution.py:84
  99.3 35.4 %collective-permute-start.5 = (bf16[3,2,2,256,384]{4,3,2,1,0:T(8,128)(2,1)}, bf16[3,2,2,256,384]{4,3,2,1,0:T(8,128)(2,1)}, u32[]{:S(2)}, u32[]{:S(2)}) collective-permute-start(bf16[3,2,2,256,384]{4,3,2,1,0:T(8,128)(2,1)} %pad_maximum_fusion.2), channel_id=1, source_target_pairs={{0,4},{4,0},{8,12},{12,8},{16,20},{20,16},{24,28},{28,24},{1,5},{5... | collective-permute-start | bytes 7077896 | tf_op jit(solution)/shard_map/ppermute | solution.py:95
  102.9 11.1 %collective-permute-start.14 = (bf16[2,2,256,384]{3,2,1,0:T(8,128)(2,1)}, bf16[2,2,256,384]{3,2,1,0:T(8,128)(2,1)}, u32[]{:S(2)}, u32[]{:S(2)}) collective-permute-start(bf16[2,2,256,384]{3,2,1,0:T(8,128)(2,1)} %add_convert_fusion.4), channel_id=1, source_target_pairs={{0,8},{8,16},{16,24},{28,20},{20,12},{12,4},{1,9},{9,17},{17,25},{... | collective-permute-start | bytes 2359304 | tf_op jit(solution)/shard_map/ppermute | solution.py:84
  107.0 39.3 %collective-permute-start.16 = (bf16[3,2,2,256,384]{4,3,2,1,0:T(8,128)(2,1)S(1)}, bf16[3,2,2,256,384]{4,3,2,1,0:T(8,128)(2,1)S(1)}, u32[]{:S(2)}, u32[]{:S(2)}) collective-permute-start(bf16[3,2,2,256,384]{4,3,2,1,0:T(8,128)(2,1)S(1)} %pad_maximum_fusion.4), channel_id=1, source_target_pairs={{0,4},{4,0},{8,12},{12,8},{16,20},{20,16},{24,28},{28,24},{1,5},{5... | collective-permute-start | bytes 7077896 | tf_op jit(solution)/shard_map/ppermute | solution.py:95
  108.6 8.2 %collective-permute-start.4 = (bf16[2,2,256,384]{3,2,1,0:T(8,128)(2,1)S(1)}, bf16[2,2,256,384]{3,2,1,0:T(8,128)(2,1)S(1)}, u32[]{:S(2)}, u32[]{:S(2)}) collective-permute-start(bf16[2,2,256,384]{3,2,1,0:T(8,128)(2,1)S(1)} %fusion.38), channel_id=1, source_target_pairs={{0,4},{4,0},{8,12},{12,8},{16,20},{20,16},{24,28},{28,24},{1,5},{5... | collective-permute-start | bytes 2359304 | tf_op jit(solution)/shard_map/ppermute | solution.py:147
  115.3 17.1 %collective-permute-start.15 = (bf16[2,2,256,384]{3,2,1,0:T(8,128)(2,1)S(1)}, bf16[2,2,256,384]{3,2,1,0:T(8,128)(2,1)S(1)}, u32[]{:S(2)}, u32[]{:S(2)}) collective-permute-start(bf16[2,2,256,384]{3,2,1,0:T(8,128)(2,1)S(1)} %fusion.31), channel_id=1, source_target_pairs={{0,4},{4,0},{8,12},{12,8},{16,20},{20,16},{24,28},{28,24},{1,5},{5... | collective-permute-start | bytes 2359304 | tf_op jit(solution)/shard_map/ppermute | solution.py:147
  116.8 17.9 %copy-start.7 = (bf16[2,2048,384]{2,1,0:T(8,128)(2,1)S(1)}, bf16[2,2048,384]{2,1,0:T(8,128)(2,1)}, u32[]{:S(2)}) copy-start(bf16[2,2048,384]{2,1,0:T(8,128)(2,1)} %copy.27) | copy-start | bytes 9437188
  117.0 24.8 %collective-permute-start.6 = (bf16[2,2,256,384]{3,2,1,0:T(8,128)(2,1)S(1)}, bf16[2,2,256,384]{3,2,1,0:T(8,128)(2,1)S(1)}, u32[]{:S(2)}, u32[]{:S(2)}) collective-permute-start(bf16[2,2,256,384]{3,2,1,0:T(8,128)(2,1)S(1)} %add_convert_fusion.10.refs_0_), channel_id=1, source_target_pairs={{0,8},{8,16},{16,24},{28,20},{20,12},{12,4},{1,9},{9,17},{17,25},{... | collective-permute-start | bytes 2359304 | tf_op jit(solution)/shard_map/ppermute | solution.py:84
  132.4 13.9 %copy-start.5 = (bf16[2,2048,384]{2,1,0:T(8,128)(2,1)S(1)}, bf16[2,2048,384]{2,1,0:T(8,128)(2,1)}, u32[]{:S(2)}) copy-start(bf16[2,2048,384]{2,1,0:T(8,128)(2,1)} %copy-done.4) | copy-start | bytes 9437188
  132.6 17.6 %collective-permute-start.17 = (bf16[2,2,256,384]{3,2,1,0:T(8,128)(2,1)S(1)}, bf16[2,2,256,384]{3,2,1,0:T(8,128)(2,1)S(1)}, u32[]{:S(2)}, u32[]{:S(2)}) collective-permute-start(bf16[2,2,256,384]{3,2,1,0:T(8,128)(2,1)S(1)} %add_convert_fusion.3.refs_4_), channel_id=1, source_target_pairs={{0,8},{8,16},{16,24},{28,20},{20,12},{12,4},{1,9},{9,17},{17,25},{... | collective-permute-start | bytes 2359304 | tf_op jit(solution)/shard_map/ppermute | solution.py:84
  141.8 16.9 %collective-permute-start.7 = (bf16[2,2,256,384]{3,2,1,0:T(8,128)(2,1)S(1)}, bf16[2,2,256,384]{3,2,1,0:T(8,128)(2,1)S(1)}, u32[]{:S(2)}, u32[]{:S(2)}) collective-permute-start(bf16[2,2,256,384]{3,2,1,0:T(8,128)(2,1)S(1)} %fusion.32), channel_id=1, source_target_pairs={{0,8},{28,20},{1,9},{29,21},{2,10},{30,22},{3,11},{31,23}} | collective-permute-start | bytes 2359304 | tf_op jit(solution)/shard_map/ppermute | solution.py:84
  150.3 16.8 %collective-permute-start.18 = (bf16[2,2,256,384]{3,2,1,0:T(8,128)(2,1)S(1)}, bf16[2,2,256,384]{3,2,1,0:T(8,128)(2,1)S(1)}, u32[]{:S(2)}, u32[]{:S(2)}) collective-permute-start(bf16[2,2,256,384]{3,2,1,0:T(8,128)(2,1)S(1)} %fusion.24), channel_id=1, source_target_pairs={{0,8},{28,20},{1,9},{29,21},{2,10},{30,22},{3,11},{31,23}} | collective-permute-start | bytes 2359304 | tf_op jit(solution)/shard_map/ppermute | solution.py:84
  160.1 15.4 %collective-permute-start.8 = (bf16[2,2,256,384]{3,2,1,0:T(8,128)(2,1)S(1)}, bf16[2,2,256,384]{3,2,1,0:T(8,128)(2,1)S(1)}, u32[]{:S(2)}, u32[]{:S(2)}) collective-permute-start(bf16[2,2,256,384]{3,2,1,0:T(8,128)(2,1)S(1)} %add_convert_fusion.9), channel_id=1, source_target_pairs={{0,8},{8,16},{28,20},{20,12},{1,9},{9,17},{29,21},{21,13},{2,10},{... | collective-permute-start | bytes 2359304 | tf_op jit(solution)/shard_map/ppermute | solution.py:84
  167.4 16.5 %collective-permute-start.19 = (bf16[2,2,256,384]{3,2,1,0:T(8,128)(2,1)S(1)}, bf16[2,2,256,384]{3,2,1,0:T(8,128)(2,1)S(1)}, u32[]{:S(2)}, u32[]{:S(2)}) collective-permute-start(bf16[2,2,256,384]{3,2,1,0:T(8,128)(2,1)S(1)} %add_convert_fusion.2), channel_id=1, source_target_pairs={{0,8},{8,16},{28,20},{20,12},{1,9},{9,17},{29,21},{21,13},{2,10},{... | collective-permute-start | bytes 2359304 | tf_op jit(solution)/shard_map/ppermute | solution.py:84
  177.9 23.8 %collective-permute-start.9 = (bf16[2,2,256,384]{3,2,1,0:T(8,128)(2,1)}, bf16[2,2,256,384]{3,2,1,0:T(8,128)(2,1)S(1)}, u32[]{:S(2)}, u32[]{:S(2)}) collective-permute-start(bf16[2,2,256,384]{3,2,1,0:T(8,128)(2,1)} %add_convert_fusion.8), channel_id=1, source_target_pairs={{0,8},{8,16},{16,24},{28,20},{20,12},{12,4},{1,9},{9,17},{17,25},{... | collective-permute-start | bytes 2359304 | tf_op jit(solution)/shard_map/ppermute | solution.py:84
  185.2 18.4 %collective-permute-start.20 = (bf16[2,2,256,384]{3,2,1,0:T(8,128)(2,1)}, bf16[2,2,256,384]{3,2,1,0:T(8,128)(2,1)S(1)}, u32[]{:S(2)}, u32[]{:S(2)}) collective-permute-start(bf16[2,2,256,384]{3,2,1,0:T(8,128)(2,1)} %add_convert_fusion.1), channel_id=1, source_target_pairs={{0,8},{8,16},{16,24},{28,20},{20,12},{12,4},{1,9},{9,17},{17,25},{... | collective-permute-start | bytes 2359304 | tf_op jit(solution)/shard_map/ppermute | solution.py:84
  203.0 38.6 %collective-permute-start.22 = (bf16[4,4,2,224,256]{4,3,2,1,0:T(8,128)(2,1)}, bf16[4,4,2,224,256]{4,3,2,1,0:T(8,128)(2,1)}, u32[]{:S(2)}, u32[]{:S(2)}) collective-permute-start(bf16[4,4,2,224,256]{4,3,2,1,0:T(8,128)(2,1)} %bitcast.282), channel_id=1, source_target_pairs={{0,4},{4,0},{8,12},{12,8},{16,20},{20,16},{24,28},{28,24},{1,5},{5... | collective-permute-start | bytes 11010056 | tf_op jit(solution)/shard_map/ppermute | solution.py:159
  203.0 7.2 %collective-permute-start.10 = (bf16[2,2,256,384]{3,2,1,0:T(8,128)(2,1)S(1)}, bf16[2,2,256,384]{3,2,1,0:T(8,128)(2,1)S(1)}, u32[]{:S(2)}, u32[]{:S(2)}) collective-permute-start(bf16[2,2,256,384]{3,2,1,0:T(8,128)(2,1)S(1)} %add_convert_fusion.7), channel_id=1, source_target_pairs={{0,4},{4,0},{8,12},{12,8},{16,20},{20,16},{24,28},{28,24},{1,5},{5... | collective-permute-start | bytes 2359304 | tf_op jit(solution)/shard_map/ppermute | solution.py:147
  204.9 8.3 %collective-permute-start.21 = (bf16[2,2,256,384]{3,2,1,0:T(8,128)(2,1)S(1)}, bf16[2,2,256,384]{3,2,1,0:T(8,128)(2,1)S(1)}, u32[]{:S(2)}, u32[]{:S(2)}) collective-permute-start(bf16[2,2,256,384]{3,2,1,0:T(8,128)(2,1)S(1)} %fusion.27), channel_id=1, source_target_pairs={{0,4},{4,0},{8,12},{12,8},{16,20},{20,16},{24,28},{28,24},{1,5},{5... | collective-permute-start | bytes 2359304 | tf_op jit(solution)/shard_map/ppermute | solution.py:147
  210.4 24.5 %copy-start.17 = (s32[56,4]{0,1:T(4,128)S(1)}, s32[56,4]{0,1:T(4,128)}, u32[]{:S(2)}) copy-start(s32[56,4]{0,1:T(4,128)} %param.11) | copy-start | bytes 2692
  210.4 24.5 %copy-start.18 = (s32[56,4,1]{0,2,1:T(1,128)S(1)}, s32[56,4,1]{0,2,1:T(1,128)}, u32[]{:S(2)}) copy-start(s32[56,4,1]{0,2,1:T(1,128)} %param.10) | copy-start | bytes 2692
  210.4 11.4 %collective-permute-start.37 = (bf16[2,2,256,384]{3,2,1,0:T(8,128)(2,1)S(1)}, bf16[2,2,256,384]{3,2,1,0:T(8,128)(2,1)}, u32[]{:S(2)}, u32[]{:S(2)}) collective-permute-start(bf16[2,2,256,384]{3,2,1,0:T(8,128)(2,1)S(1)} %add_convert_fusion.6.refs_0_), channel_id=1, source_target_pairs={{0,8},{8,16},{16,24},{28,20},{20,12},{12,4},{1,9},{9,17},{17,25},{... | collective-permute-start | bytes 2359304 | tf_op jit(solution)/shard_map/ppermute | solution.py:84
  213.4 16.8 %collective-permute-start.40 = (bf16[2,2,256,384]{3,2,1,0:T(8,128)(2,1)S(1)}, bf16[2,2,256,384]{3,2,1,0:T(8,128)(2,1)}, u32[]{:S(2)}, u32[]{:S(2)}) collective-permute-start(bf16[2,2,256,384]{3,2,1,0:T(8,128)(2,1)S(1)} %add_convert_fusion.refs_4_), channel_id=1, source_target_pairs={{0,8},{8,16},{16,24},{28,20},{20,12},{12,4},{1,9},{9,17},{17,25},{... | collective-permute-start | bytes 2359304 | tf_op jit(solution)/shard_map/ppermute | solution.py:84
  221.8 13.3 %collective-permute-start.38 = (bf16[2,2,256,384]{3,2,1,0:T(8,128)(2,1)}, bf16[2,2,256,384]{3,2,1,0:T(8,128)(2,1)}, u32[]{:S(2)}, u32[]{:S(2)}) collective-permute-start(bf16[2,2,256,384]{3,2,1,0:T(8,128)(2,1)} %collective-permute-done.37.refs_1_), channel_id=1, source_target_pairs={{8,16},{16,24},{20,12},{12,4},{9,17},{17,25},{21,13},{13,5},{10,18... | collective-permute-start | bytes 2359304 | tf_op jit(solution)/shard_map/ppermute | solution.py:84
  230.2 6.4 %collective-permute-start.41 = (bf16[2,2,256,384]{3,2,1,0:T(8,128)(2,1)}, bf16[2,2,256,384]{3,2,1,0:T(8,128)(2,1)}, u32[]{:S(2)}, u32[]{:S(2)}) collective-permute-start(bf16[2,2,256,384]{3,2,1,0:T(8,128)(2,1)} %collective-permute-done.40.refs_5_), channel_id=1, source_target_pairs={{8,16},{16,24},{20,12},{12,4},{9,17},{17,25},{21,13},{13,5},{10,18... | collective-permute-start | bytes 2359304 | tf_op jit(solution)/shard_map/ppermute | solution.py:84
  231.8 7.4 %collective-permute-start.23 = (bf16[2,2,256,384]{3,2,1,0:T(8,128)(2,1)}, bf16[2,2,256,384]{3,2,1,0:T(8,128)(2,1)}, u32[]{:S(2)}, u32[]{:S(2)}) collective-permute-start(bf16[2,2,256,384]{3,2,1,0:T(8,128)(2,1)} %copy-done), channel_id=1, source_target_pairs={{8,16},{16,24},{20,12},{12,4},{9,17},{17,25},{21,13},{13,5},{10,18... | collective-permute-start | bytes 2359304 | tf_op jit(solution)/shard_map/ppermute | solution.py:84
  233.3 6.6 %collective-permute-start.25 = (bf16[2,2,256,384]{3,2,1,0:T(8,128)(2,1)}, bf16[2,2,256,384]{3,2,1,0:T(8,128)(2,1)}, u32[]{:S(2)}, u32[]{:S(2)}) collective-permute-start(bf16[2,2,256,384]{3,2,1,0:T(8,128)(2,1)} %copy-done.2), channel_id=1, source_target_pairs={{8,16},{16,24},{20,12},{12,4},{9,17},{17,25},{21,13},{13,5},{10,18... | collective-permute-start | bytes 2359304 | tf_op jit(solution)/shard_map/ppermute | solution.py:84
  235.1 13.2 %collective-permute-start.39 = (bf16[2,2,256,384]{3,2,1,0:T(8,128)(2,1)}, bf16[2,2,256,384]{3,2,1,0:T(8,128)(2,1)}, u32[]{:S(2)}, u32[]{:S(2)}) collective-permute-start(bf16[2,2,256,384]{3,2,1,0:T(8,128)(2,1)} %collective-permute-done.38.refs_2_), channel_id=1, source_target_pairs={{16,24},{12,4},{17,25},{13,5},{18,26},{14,6},{19,27},{15,7}} | collective-permute-start | bytes 2359304 | tf_op jit(solution)/shard_map/ppermute | solution.py:84
  236.6 11.6 %collective-permute-start.42 = (bf16[2,2,256,384]{3,2,1,0:T(8,128)(2,1)}, bf16[2,2,256,384]{3,2,1,0:T(8,128)(2,1)}, u32[]{:S(2)}, u32[]{:S(2)}) collective-permute-start(bf16[2,2,256,384]{3,2,1,0:T(8,128)(2,1)} %collective-permute-done.41.refs_6_), channel_id=1, source_target_pairs={{16,24},{12,4},{17,25},{13,5},{18,26},{14,6},{19,27},{15,7}} | collective-permute-start | bytes 2359304 | tf_op jit(solution)/shard_map/ppermute | solution.py:84
  239.2 54.2 %collective-permute-start.24 = (bf16[2,2,256,384]{3,2,1,0:T(8,128)(2,1)}, bf16[2,2,256,384]{3,2,1,0:T(8,128)(2,1)S(1)}, u32[]{:S(2)}, u32[]{:S(2)}) collective-permute-start(bf16[2,2,256,384]{3,2,1,0:T(8,128)(2,1)} %collective-permute-done.23.refs_2_), channel_id=1, source_target_pairs={{16,24},{12,4},{17,25},{13,5},{18,26},{14,6},{19,27},{15,7}} | collective-permute-start | bytes 2359304 | tf_op jit(solution)/shard_map/ppermute | solution.py:84
  240.0 53.5 %collective-permute-start.26 = (bf16[2,2,256,384]{3,2,1,0:T(8,128)(2,1)}, bf16[2,2,256,384]{3,2,1,0:T(8,128)(2,1)}, u32[]{:S(2)}, u32[]{:S(2)}) collective-permute-start(bf16[2,2,256,384]{3,2,1,0:T(8,128)(2,1)} %collective-permute-done.25.refs_6_), channel_id=1, source_target_pairs={{16,24},{12,4},{17,25},{13,5},{18,26},{14,6},{19,27},{15,7}} | collective-permute-start | bytes 2359304 | tf_op jit(solution)/shard_map/ppermute | solution.py:84
  248.3 45.2 %copy-start.3 = (bf16[2,2,256,384]{3,2,1,0:T(8,128)(2,1)S(1)}, bf16[2,2,256,384]{3,2,1,0:T(8,128)(2,1)}, u32[]{:S(2)}) copy-start(bf16[2,2,256,384]{3,2,1,0:T(8,128)(2,1)} %copy-done.2) | copy-start | bytes 2359300
  257.8 35.7 %copy-start.1 = (bf16[2,2,256,384]{3,2,1,0:T(8,128)(2,1)S(1)}, bf16[2,2,256,384]{3,2,1,0:T(8,128)(2,1)}, u32[]{:S(2)}) copy-start(bf16[2,2,256,384]{3,2,1,0:T(8,128)(2,1)} %copy-done) | copy-start | bytes 2359300
  259.0 51.9 %collective-permute-start.43 = (bf16[4,7,4,8,384]{4,3,2,1,0:T(8,128)(2,1)S(1)}, bf16[4,7,4,8,384]{4,3,2,1,0:T(8,128)(2,1)S(1)}, u32[]{:S(2)}, u32[]{:S(2)}) collective-permute-start(bf16[4,7,4,8,384]{4,3,2,1,0:T(8,128)(2,1)S(1)} %dynamic-slice_bitcast_fusion.13), channel_id=1, source_target_pairs={{0,4},{4,0},{8,12},{12,8},{16,20},{20,16},{24,28},{28,24},{1,5},{5... | collective-permute-start | bytes 2064392 | tf_op jit(solution)/shard_map/ppermute | solution.py:102
  303.4 11.9 %collective-permute-start.27 = (bf16[4,7,4,8,384]{4,3,2,1,0:T(8,128)(2,1)S(1)}, bf16[4,7,4,8,384]{4,3,2,1,0:T(8,128)(2,1)S(1)}, u32[]{:S(2)}, u32[]{:S(2)}) collective-permute-start(bf16[4,7,4,8,384]{4,3,2,1,0:T(8,128)(2,1)S(1)} %dynamic-slice_bitcast_fusion.14), channel_id=1, source_target_pairs={{0,4},{4,0},{8,12},{12,8},{16,20},{20,16},{24,28},{28,24},{1,5},{5... | collective-permute-start | bytes 2064392 | tf_op jit(solution)/shard_map/ppermute | solution.py:102
  311.7 8.2 %collective-permute-start.46 = (bf16[4,7,8,384]{3,2,1,0:T(8,128)(2,1)S(1)}, bf16[4,7,8,384]{3,2,1,0:T(8,128)(2,1)S(1)}, u32[]{:S(2)}, u32[]{:S(2)}) collective-permute-start(bf16[4,7,8,384]{3,2,1,0:T(8,128)(2,1)S(1)} %get-tuple-element.40), channel_id=1, source_target_pairs={{0,3},{1,2},{2,1},{3,0},{4,7},{5,6},{6,5},{7,4},{8,11},{9,10},{10,... | collective-permute-start | bytes 516104 | tf_op jit(solution)/shard_map/ppermute | solution.py:106
  314.3 9.5 %collective-permute-start.45 = (bf16[4,7,8,384]{3,2,1,0:T(8,128)(2,1)S(1)}, bf16[4,7,8,384]{3,2,1,0:T(8,128)(2,1)S(1)}, u32[]{:S(2)}, u32[]{:S(2)}) collective-permute-start(bf16[4,7,8,384]{3,2,1,0:T(8,128)(2,1)S(1)} %get-tuple-element.41), channel_id=1, source_target_pairs={{0,2},{1,3},{2,0},{3,1},{4,6},{5,7},{6,4},{7,5},{8,10},{9,11},{10,... | collective-permute-start | bytes 516104 | tf_op jit(solution)/shard_map/ppermute | solution.py:106
  314.8 9.0 %collective-permute-start.44 = (bf16[4,7,8,384]{3,2,1,0:T(8,128)(2,1)S(1)}, bf16[4,7,8,384]{3,2,1,0:T(8,128)(2,1)S(1)}, u32[]{:S(2)}, u32[]{:S(2)}) collective-permute-start(bf16[4,7,8,384]{3,2,1,0:T(8,128)(2,1)S(1)} %get-tuple-element.39), channel_id=1, source_target_pairs={{0,1},{1,0},{2,3},{3,2},{4,5},{5,4},{6,7},{7,6},{8,9},{9,8},{10,11... | collective-permute-start | bytes 516104 | tf_op jit(solution)/shard_map/ppermute | solution.py:106
  315.6 11.8 %collective-permute-start.30 = (bf16[4,7,8,384]{3,2,1,0:T(8,128)(2,1)S(1)}, bf16[4,7,8,384]{3,2,1,0:T(8,128)(2,1)S(1)}, u32[]{:S(2)}, u32[]{:S(2)}) collective-permute-start(bf16[4,7,8,384]{3,2,1,0:T(8,128)(2,1)S(1)} %get-tuple-element.37), channel_id=1, source_target_pairs={{0,3},{1,2},{2,1},{3,0},{4,7},{5,6},{6,5},{7,4},{8,11},{9,10},{10,... | collective-permute-start | bytes 516104 | tf_op jit(solution)/shard_map/ppermute | solution.py:106
  318.1 12.0 %collective-permute-start.29 = (bf16[4,7,8,384]{3,2,1,0:T(8,128)(2,1)S(1)}, bf16[4,7,8,384]{3,2,1,0:T(8,128)(2,1)S(1)}, u32[]{:S(2)}, u32[]{:S(2)}) collective-permute-start(bf16[4,7,8,384]{3,2,1,0:T(8,128)(2,1)S(1)} %get-tuple-element.38), channel_id=1, source_target_pairs={{0,2},{1,3},{2,0},{3,1},{4,6},{5,7},{6,4},{7,5},{8,10},{9,11},{10,... | collective-permute-start | bytes 516104 | tf_op jit(solution)/shard_map/ppermute | solution.py:106
  319.9 10.3 %collective-permute-start.28 = (bf16[4,7,8,384]{3,2,1,0:T(8,128)(2,1)S(1)}, bf16[4,7,8,384]{3,2,1,0:T(8,128)(2,1)S(1)}, u32[]{:S(2)}, u32[]{:S(2)}) collective-permute-start(bf16[4,7,8,384]{3,2,1,0:T(8,128)(2,1)S(1)} %get-tuple-element.36), channel_id=1, source_target_pairs={{0,1},{1,0},{2,3},{3,2},{4,5},{5,4},{6,7},{7,6},{8,9},{9,8},{10,11... | collective-permute-start | bytes 516104 | tf_op jit(solution)/shard_map/ppermute | solution.py:106
  323.8 21.5 %copy-start.16 = (f32[224,768]{1,0:T(8,128)S(1)}, f32[224,768]{1,0:T(8,128)}, u32[]{:S(2)}) copy-start(f32[224,768]{1,0:T(8,128)} %param.9) | copy-start | bytes 2064388
  323.9 7.8 %collective-permute-start.49 = (bf16[7,8,384]{2,1,0:T(8,128)(2,1)S(1)}, bf16[7,8,384]{2,1,0:T(8,128)(2,1)S(1)}, u32[]{:S(2)}, u32[]{:S(2)}) collective-permute-start(bf16[7,8,384]{2,1,0:T(8,128)(2,1)S(1)} %get-tuple-element.46), channel_id=1, source_target_pairs={{0,24},{4,28},{8,0},{12,4},{16,8},{20,12},{24,16},{28,20},{1,25},{... | collective-permute-start | bytes 129032 | tf_op jit(solution)/shard_map/ppermute | solution.py:113
  324.0 8.4 %collective-permute-start.48 = (bf16[7,8,384]{2,1,0:T(8,128)(2,1)S(1)}, bf16[7,8,384]{2,1,0:T(8,128)(2,1)S(1)}, u32[]{:S(2)}, u32[]{:S(2)}) collective-permute-start(bf16[7,8,384]{2,1,0:T(8,128)(2,1)S(1)} %get-tuple-element.47), channel_id=1, source_target_pairs={{0,16},{4,20},{8,24},{12,28},{16,0},{20,4},{24,8},{28,12},{1,17},{... | collective-permute-start | bytes 129032 | tf_op jit(solution)/shard_map/ppermute | solution.py:113
  327.4 5.8 %collective-permute-start.47 = (bf16[7,8,384]{2,1,0:T(8,128)(2,1)S(1)}, bf16[7,8,384]{2,1,0:T(8,128)(2,1)S(1)}, u32[]{:S(2)}, u32[]{:S(2)}) collective-permute-start(bf16[7,8,384]{2,1,0:T(8,128)(2,1)S(1)} %get-tuple-element.45), channel_id=1, source_target_pairs={{0,8},{4,12},{8,16},{12,20},{16,24},{20,28},{24,0},{28,4},{1,9},{5... | collective-permute-start | bytes 129032 | tf_op jit(solution)/shard_map/ppermute | solution.py:113
  330.4 6.1 %collective-permute-start.33 = (bf16[7,8,384]{2,1,0:T(8,128)(2,1)S(1)}, bf16[7,8,384]{2,1,0:T(8,128)(2,1)S(1)}, u32[]{:S(2)}, u32[]{:S(2)}) collective-permute-start(bf16[7,8,384]{2,1,0:T(8,128)(2,1)S(1)} %get-tuple-element.43), channel_id=1, source_target_pairs={{0,24},{4,28},{8,0},{12,4},{16,8},{20,12},{24,16},{28,20},{1,25},{... | collective-permute-start | bytes 129032 | tf_op jit(solution)/shard_map/ppermute | solution.py:113
  331.4 5.5 %collective-permute-start.32 = (bf16[7,8,384]{2,1,0:T(8,128)(2,1)S(1)}, bf16[7,8,384]{2,1,0:T(8,128)(2,1)S(1)}, u32[]{:S(2)}, u32[]{:S(2)}) collective-permute-start(bf16[7,8,384]{2,1,0:T(8,128)(2,1)S(1)} %get-tuple-element.44), channel_id=1, source_target_pairs={{0,16},{4,20},{8,24},{12,28},{16,0},{20,4},{24,8},{28,12},{1,17},{... | collective-permute-start | bytes 129032 | tf_op jit(solution)/shard_map/ppermute | solution.py:113
  331.7 5.8 %collective-permute-start.31 = (bf16[7,8,384]{2,1,0:T(8,128)(2,1)S(1)}, bf16[7,8,384]{2,1,0:T(8,128)(2,1)S(1)}, u32[]{:S(2)}, u32[]{:S(2)}) collective-permute-start(bf16[7,8,384]{2,1,0:T(8,128)(2,1)S(1)} %get-tuple-element.42), channel_id=1, source_target_pairs={{0,8},{4,12},{8,16},{12,20},{16,24},{20,28},{24,0},{28,4},{1,9},{5... | collective-permute-start | bytes 129032 | tf_op jit(solution)/shard_map/ppermute | solution.py:113
  333.3 7.1 %collective-permute-start.50 = (bf16[7,8,384]{2,1,0:T(8,128)(2,1)S(1)}, bf16[7,8,384]{2,1,0:T(8,128)(2,1)S(1)}, u32[]{:S(2)}, u32[]{:S(2)}) collective-permute-start(bf16[7,8,384]{2,1,0:T(8,128)(2,1)S(1)} %get-tuple-element.17), channel_id=1, source_target_pairs={{0,1},{1,0},{2,3},{3,2},{4,5},{5,4},{6,7},{7,6},{8,9},{9,8},{10,11... | collective-permute-start | bytes 129032 | tf_op jit(solution)/shard_map/ppermute | solution.py:118
  334.9 6.3 %collective-permute-start.51 = (bf16[7,8,384]{2,1,0:T(8,128)(2,1)S(1)}, bf16[7,8,384]{2,1,0:T(8,128)(2,1)S(1)}, u32[]{:S(2)}, u32[]{:S(2)}) collective-permute-start(bf16[7,8,384]{2,1,0:T(8,128)(2,1)S(1)} %get-tuple-element.17), channel_id=1, source_target_pairs={{0,2},{1,3},{2,0},{3,1},{4,6},{5,7},{6,4},{7,5},{8,10},{9,11},{10,... | collective-permute-start | bytes 129032 | tf_op jit(solution)/shard_map/ppermute | solution.py:118
  336.5 5.1 %collective-permute-start.52 = (bf16[7,8,384]{2,1,0:T(8,128)(2,1)S(1)}, bf16[7,8,384]{2,1,0:T(8,128)(2,1)S(1)}, u32[]{:S(2)}, u32[]{:S(2)}) collective-permute-start(bf16[7,8,384]{2,1,0:T(8,128)(2,1)S(1)} %get-tuple-element.17), channel_id=1, source_target_pairs={{0,3},{1,2},{2,1},{3,0},{4,7},{5,6},{6,5},{7,4},{8,11},{9,10},{10,... | collective-permute-start | bytes 129032 | tf_op jit(solution)/shard_map/ppermute | solution.py:118
  337.6 4.1 %collective-permute-start.34 = (bf16[7,8,384]{2,1,0:T(8,128)(2,1)S(1)}, bf16[7,8,384]{2,1,0:T(8,128)(2,1)S(1)}, u32[]{:S(2)}, u32[]{:S(2)}) collective-permute-start(bf16[7,8,384]{2,1,0:T(8,128)(2,1)S(1)} %get-tuple-element.15), channel_id=1, source_target_pairs={{0,1},{1,0},{2,3},{3,2},{4,5},{5,4},{6,7},{7,6},{8,9},{9,8},{10,11... | collective-permute-start | bytes 129032 | tf_op jit(solution)/shard_map/ppermute | solution.py:118
  339.2 4.0 %collective-permute-start.35 = (bf16[7,8,384]{2,1,0:T(8,128)(2,1)S(1)}, bf16[7,8,384]{2,1,0:T(8,128)(2,1)S(1)}, u32[]{:S(2)}, u32[]{:S(2)}) collective-permute-start(bf16[7,8,384]{2,1,0:T(8,128)(2,1)S(1)} %get-tuple-element.15), channel_id=1, source_target_pairs={{0,2},{1,3},{2,0},{3,1},{4,6},{5,7},{6,4},{7,5},{8,10},{9,11},{10,... | collective-permute-start | bytes 129032 | tf_op jit(solution)/shard_map/ppermute | solution.py:118
  340.4 4.9 %collective-permute-start.36 = (bf16[7,8,384]{2,1,0:T(8,128)(2,1)S(1)}, bf16[7,8,384]{2,1,0:T(8,128)(2,1)S(1)}, u32[]{:S(2)}, u32[]{:S(2)}) collective-permute-start(bf16[7,8,384]{2,1,0:T(8,128)(2,1)S(1)} %get-tuple-element.15), channel_id=1, source_target_pairs={{0,3},{1,2},{2,1},{3,0},{4,7},{5,6},{6,5},{7,4},{8,11},{9,10},{10,... | collective-permute-start | bytes 129032 | tf_op jit(solution)/shard_map/ppermute | solution.py:118
  (8 other events, 38.0 us)
where the time goes:
time: 350 us; the launch traced here: 346 us
  starting transfers between devices  143 us (41%)
  waiting for transfers between devices  64.9 us (19%)
  other arithmetic  44.8 us (13%)
  local copies, waits for them, and re-layouts  38.6 us (11%)
  matrix products  35.7 us (10%)
  Pallas kernels  18.2 us (5%)
    ppermute x24, starting transfers between devices, hop(): return lax.ppermute(value, 'row', up + down)  79.9 us
    ppermute x24, waiting for transfers between devices, hop(): return lax.ppermute(value, 'row', up + down)  44.8 us
    ppermute x2, starting transfers between devices, share(): lax.ppermute(pick(total, 1 - core, 1), 'row', pair)  40.5 us
    dot_general x4, matrix products, product(): jnp.einsum('swk,skn->swn', inv_diag[s * per:(s + 1) * per], part, preferr...  35.7 us
    convert_element_type x24, other arithmetic, add16(): functools.reduce(lambda a, b: a + b, [t.astype(F32) for t in terms])  28.4 us
    pallas_call x2, Pallas kernels, apply_update(): pl.pallas_call(update_kernel, out_shape=jax.ShapeDtypeStruct((anc_blocks,...  18.2 us
    convert_element_type x3, local copies, waits for them, and re-layouts, product(): terms = jnp.einsum('swk,skn->swn', inv_diag[s * per:(s + 1) * per], part,...  12.3 us
    reshape x2, local copies, waits for them, and re-layouts, per_device(): off_diag.reshape(SNODES, off_diag.shape[1], nz, 2, own_rows)  12 us
  transfers between devices with their start and end apart: 53, of which 23 were waited for; matrix products, arithmetic and copies ran while one was open for 24% of the time, Pallas kernels for 5%

commit v1 on v0

v1 whole, which is shorter than its diff:
```python
import functools

import jax
import jax.numpy as jnp
from jax import lax
from jax.experimental import pallas as pl
from jax.experimental.pallas import tpu as pltpu
from jax.sharding import PartitionSpec as P

SNODES = 4
BLOCK = 32
HALVES = 2
STREAMS = 2
F32 = jnp.float32
BF16 = jnp.bfloat16


def add16(*terms):
    return functools.reduce(lambda a, b: a + b, [t.astype(F32) for t in terms]).astype(BF16)


def pick(array, index, axis):
    return lax.dynamic_index_in_dim(array, index, axis, keepdims=False)


def after(value, *earlier):
    return lax.optimization_barrier((value,) + earlier)[0]


def product_kernel(meta_ref, tile_ref, rhs_ref, away_ref, keep_ref):
    terms = jnp.dot(tile_ref[0, 0], rhs_ref[0], preferred_element_type=F32).astype(BF16)
    is_away = pl.program_id(1) < meta_ref[2]

    @pl.when(is_away)
    def _():
        away_ref[0, 0] = terms

    @pl.when(jnp.logical_not(is_away))
    def _():
        keep_ref[0, 0] = terms


def apply_product(meta, tiles, rhs, first, per, n, width):
    nz, rows, depth = tiles.shape[1:]

    def tile_map(s, k, meta):
        j = k - meta[2]
        return first + s, meta[0] + meta[1] * jnp.where(j < 0, -1 - k, j), 0, 0

    def away_map(s, k, meta):
        return jnp.maximum(jnp.minimum(k, meta[2] - 1), 0), s, 0, 0

    def keep_map(s, k, meta):
        return jnp.maximum(k - meta[2], 0), s, 0, 0

    block = (1, 1, rows, width)
    return pl.pallas_call(
        product_kernel,
        grid_spec=pltpu.PrefetchScalarGridSpec(
            num_scalar_prefetch=1,
            grid=(per, nz),
            in_specs=[
                pl.BlockSpec((1, 1, rows, depth), tile_map),
                pl.BlockSpec((1, depth, width), lambda s, k, meta: (first + s, 0, n)),
            ],
            out_specs=[pl.BlockSpec(block, away_map), pl.BlockSpec(block, keep_map)],
        ),
        out_shape=[
            jax.ShapeDtypeStruct((nz - 1, per, rows, width), BF16),
            jax.ShapeDtypeStruct((nz, per, rows, width), BF16),
        ],
        compiler_params=pltpu.CompilerParams(vmem_limit_bytes=32 * 1024 * 1024),
        cost_estimate=pl.CostEstimate(
            flops=2 * per * nz * rows * depth * width,
            bytes_accessed=2 * per * (nz * rows * (depth + width) + depth * width),
            transcendentals=0,
        ),
    )(meta, tiles, rhs)


def update_kernel(table_ref, meta_ref, mine_ref, theirs_ref, *refs):
    pieces, out_ref, total = refs[:-2], refs[-2], refs[-1]
    per = pieces[0].shape[0]
    rows = pieces[0].shape[1]
    nz = len(pieces) * per // SNODES
    z, side = meta_ref[0], meta_ref[1]
    core = (1 - side) // 2
    height = mine_ref.shape[-2]
    blocks = 2 * height // BLOCK

    def factor(s, start, count):
        if len(mine_ref.shape) == 3:
            at = pl.ds(pl.multiple_of(start * count, count), count)
            return jnp.concatenate([mine_ref[s, :, at], theirs_ref[s, :, at]], axis=0)
        per_index = rows // count
        both = jnp.concatenate([mine_ref[s, start // per_index], theirs_ref[s, start // per_index]], axis=0)
        if per_index == 1:
            return both
        return jnp.where(core == 0, both[:, :count], both[:, count:])

    total[...] = jnp.zeros_like(total)
    half = rows // 2
    for s in range(SNODES):
        own = pieces[(s // per) * nz]
        part = jnp.dot(
            factor(s, 2 * z + core, half),
            own[s % per, pl.ds(pl.multiple_of(core * half, half), half)],
            preferred_element_type=F32,
        )
        for t in range(1, nz):
            chip = jnp.clip(z - side * t, 0, nz - 1)
            part += jnp.dot(
                factor(s, chip, rows), pieces[(s // per) * nz + t][s % per], preferred_element_type=F32
            )
        for b in range(blocks):
            total[table_ref[s * blocks + b]] += part[b * BLOCK : (b + 1) * BLOCK]
    out_ref[...] = total[...].astype(out_ref.dtype)


def apply_update(table, meta, mine, theirs, pieces, anc_blocks):
    width = pieces[0].shape[-1]
    return pl.pallas_call(
        update_kernel,
        out_shape=jax.ShapeDtypeStruct((anc_blocks, BLOCK, width), BF16),
        in_specs=[pl.BlockSpec(memory_space=pltpu.SMEM)] * 2
        + [pl.BlockSpec(memory_space=pltpu.VMEM)] * (2 + len(pieces)),
        out_specs=pl.BlockSpec(memory_space=pltpu.VMEM),
        scratch_shapes=[pltpu.VMEM((anc_blocks, BLOCK, width), F32)],
        compiler_params=pltpu.CompilerParams(vmem_limit_bytes=48 * 1024 * 1024),
        cost_estimate=pl.CostEstimate(
            flops=4 * mine.size * width,
            bytes_accessed=mine.size * 4 + anc_blocks * BLOCK * width * 2,
            transcendentals=0,
        ),
    )(table, meta, mine, theirs, *pieces)


def per_device(inv_diag, off_diag, rhs, anc_rhs, dest_device, dest_slot):
    n_row, n_col = lax.axis_size("row"), lax.axis_size("col")
    nz = n_row // 2
    row, col = lax.axis_index("row"), lax.axis_index("col")
    z, core = row // 2, row % 2
    side = 1 - 2 * core
    own_rows = inv_diag.shape[1] // n_row
    anc_dev = anc_rhs.shape[0] // BLOCK
    anc_blocks = n_row * anc_dev
    width = rhs.shape[2] // HALVES
    per = SNODES // STREAMS
    pair = [(r, r ^ 1) for r in range(n_row)]

    def hop(value, sources):
        up = [(2 * i, 2 * i + 2) for i in sources if i + 1 < nz]
        down = [(2 * (nz - 1 - i) + 1, 2 * (nz - 2 - i) + 1) for i in sources if i + 1 < nz]
        return lax.ppermute(value, "row", up + down)

    tiles = inv_diag.reshape(SNODES, nz, 2 * own_rows, inv_diag.shape[2])
    meta = jnp.stack([z, side, jnp.where(core == 0, z, nz - 1 - z)]).astype(jnp.int32)

    def product(s, n, *earlier):
        return apply_product(after(meta, *earlier), tiles, rhs, s * per, per, n, width)

    def sum_cores(terms):
        away, keep = terms
        other = lax.ppermute(away, "row", pair)
        return [(keep[0],)] + [(keep[j], other[j - 1]) for j in range(1, nz)]

    turns = [[(i, i ^ d) for i in range(n_col)] for d in range(1, n_col)]
    moves = [[(2 * i + q, 2 * ((i + d) % nz) + q) for i in range(nz) for q in range(2)] for d in range(1, nz)]

    def share_cores(total):
        total = total.reshape(nz, 2, anc_dev, n_col, BLOCK // n_col, width)
        return add16(pick(total, core, 1), lax.ppermute(pick(total, 1 - core, 1), "row", pair))

    def share_col(total):
        return add16(
            pick(total, col, 2),
            *[lax.ppermute(pick(total, col ^ d, 2), "col", turns[d - 1]) for d in range(1, n_col)],
        )

    def share_line(total):
        return add16(
            pick(total, z, 0),
            *[lax.ppermute(pick(total, (z + d) % nz, 0), "row", moves[d - 1]) for d in range(1, nz)],
        )

    def share_out(total):
        whole = jnp.zeros((anc_dev, n_col) + total.shape[1:], BF16)
        whole = lax.dynamic_update_index_in_dim(whole, total, col, 1)
        for d in range(1, n_col):
            other = lax.ppermute(total, "col", turns[d - 1])
            whole = lax.dynamic_update_index_in_dim(whole, other, col ^ d, 1)
        return whole.reshape(anc_dev * BLOCK, width)

    shares = [share_cores, share_col, share_line, share_out]

    per_dev = off_diag.shape[1] // BLOCK
    target = (dest_device[:, :, 0] * anc_dev + dest_slot).reshape(n_row, per_dev, SNODES)
    table = jnp.concatenate([pick(target, row, 0), pick(target, row ^ 1, 0)], axis=0).T.reshape(-1)
    split = (lambda x: x) if (own_rows % 128 == 0) else (
        lambda x: x.reshape(SNODES, x.shape[1], nz, 2 * own_rows).transpose(0, 2, 1, 3)
    )

    terms = [[None] * HALVES for _ in range(STREAMS)]
    for s in range(STREAMS):
        terms[s][0] = product(s, 0, *(terms[s - 1][0] if s else ()))
    for s in range(STREAMS):
        terms[s][0] = sum_cores(terms[s][0])

    own = [[None] * HALVES for _ in range(STREAMS)]
    pieces = [[None] * HALVES for _ in range(STREAMS)]
    flows = [()] * STREAMS
    for t in range(1, nz):
        for s in range(STREAMS):
            flows[s] = (hop(add16(*terms[s][0][nz - t], *flows[s]), range(t)),)
            if t == 1:
                for n in range(1, HALVES):
                    terms[s][n] = sum_cores(product(s, n, flows[s][0]))
        if t == nz - 1:
            theirs = lax.ppermute(after(off_diag, flows[0][0]), "row", pair)
    mine, theirs = split(off_diag), split(theirs)

    total, totals = None, []
    for n in range(HALVES):
        partial = [add16(*terms[s][n][0], *flows[s]) for s in range(STREAMS)]
        if total is not None:
            partial[0] = after(partial[0], total)
        for s in range(STREAMS):
            own[s][n] = add16(partial[s], lax.ppermute(partial[s], "row", pair))
        flows = [()] * STREAMS
        got = [[own[s][n]] for s in range(STREAMS)]
        for t in range(1, nz + 1):
            for s in range(STREAMS):
                if t < nz:
                    send = got[s][-1]
                    if total is not None and s == 0 and t <= len(shares):
                        total = shares[t - 1](total)
                        send = after(send, total) if t > 1 else send
                    got[s].append(hop(send, range(t - 1, nz)))
                if t > 1 and n + 1 < HALVES:
                    send = add16(*terms[s][n + 1][nz - t + 1], *flows[s])
                    if t == 2:
                        send = after(send, got[s][1])
                    flows[s] = (hop(send, range(t - 1)),)
        if total is not None:
            for stage in shares[nz - 1 :]:
                total = stage(total)
            totals.append(total)
        flat = [p for s in range(STREAMS) for p in got[s]]
        total = apply_update(table, meta, mine, theirs, flat, anc_blocks)
    for stage in shares:
        total = stage(total)
    totals.append(total)
    solution = jnp.concatenate(
        [jnp.concatenate(
                [lax.dynamic_slice_in_dim(own[s][n], core * own_rows, own_rows, 1) for n in range(HALVES)], axis=2
            ) for s in range(STREAMS)],
        axis=0,
    )
    anc_out = anc_rhs - jnp.concatenate(totals, axis=1).astype(F32)
    return (solution, anc_out)


def solution(mesh):
    in_specs = (
        P(None, "col", "row"),
        P(None, "row", "col"),
        P(None, "row", None),
        P("row", None),
        P(),
        P(),
    )
    out_specs = (P(None, ("col", "row"), None), P("row", None))
    return jax.shard_map(
        per_device, mesh=mesh, in_specs=in_specs, out_specs=out_specs, check_vma=False
    )
```

time: 350 us -> 288 us (0.82)
  Pallas kernels: 18.2 us -> 56.6 us
  matrix products: 35.7 us -> 0 us
  local copies, waits for them, and re-layouts: 38.6 us -> 9.75 us
  other arithmetic: 44.8 us -> 20.3 us
  waiting for transfers between devices: 64.9 us -> 53.3 us
    pallas_call x0 -> x4, Pallas kernels: none -> 38.3 us  [apply_product(): pl.pallas_call(product_kernel, grid_spec=pltpu.PrefetchScalarGridSpec(num...]
    dot_general x4 -> x0, matrix products: 35.7 us -> none  [product(): jnp.einsum('swk,skn->swn', inv_diag[s * per:(s + 1) * per], part, preferr...]
    ppermute x24, waiting for transfers between devices: 44.8 us -> 26 us  [hop(): return lax.ppermute(value, 'row', up + down)]
    convert_element_type x3 -> x0, local copies, waits for them, and re-layouts: 12.3 us -> none  [product(): terms = jnp.einsum('swk,skn->swn', inv_diag[s * per:(s + 1) * per], part,...]
    reshape x2 -> x0, local copies, waits for them, and re-layouts: 12 us -> none  [per_device(): off_diag.reshape(SNODES, off_diag.shape[1], nz, 2, own_rows)]
    convert_element_type x24, other arithmetic: 28.4 us -> 17 us  [add16(): functools.reduce(lambda a, b: a + b, [t.astype(F32) for t in terms])]
    ppermute x25, waiting for transfers between devices: 19.4 us -> 27.3 us  [the longest x6 13.6 us: share_col(): lax.ppermute(pick(total, col ^ d, 2), 'col', turns[d - 1])]
    another operation x5 -> x1, other arithmetic: 7.26 us -> 0.08 us  [per_device(): jnp.stack([z, side, jnp.where(core == 0, z, nz - 1 - z)]).astype(jnp.int32)]
  transfers between devices with their start and end apart: 53 -> 53, of which waited for: 23 -> 24; matrix products, arithmetic and copies ran while one was open for 24% -> 8% of each run, Pallas kernels for 5% -> 13%
where the time goes in v1:
time: 288 us; the launch traced here: 286 us
  starting transfers between devices  145 us (50%)
  Pallas kernels  56.6 us (20%)
  waiting for transfers between devices  53.3 us (19%)
  other arithmetic  20.3 us (7%)
  local copies, waits for them, and re-layouts  9.75 us (3%)
    ppermute x24, starting transfers between devices, hop(): return lax.ppermute(value, 'row', up + down)  85.6 us
    pallas_call x4, Pallas kernels, apply_product(): pl.pallas_call(product_kernel, grid_spec=pltpu.PrefetchScalarGridSpec(num...  38.3 us
    ppermute x24, waiting for transfers between devices, hop(): return lax.ppermute(value, 'row', up + down)  26 us
    ppermute x2, starting transfers between devices, share_cores(): lax.ppermute(pick(total, 1 - core, 1), 'row', pair)  25.3 us
    pallas_call x2, Pallas kernels, apply_update(): pl.pallas_call(update_kernel, out_shape=jax.ShapeDtypeStruct((anc_blocks,...  18.3 us
    convert_element_type x24, other arithmetic, add16(): functools.reduce(lambda a, b: a + b, [t.astype(F32) for t in terms])  17 us
    ppermute x6, starting transfers between devices, share_line(): lax.ppermute(pick(total, (z + d) % nz, 0), 'row', moves[d - 1])  16.4 us
    ppermute x6, waiting for transfers between devices, share_col(): lax.ppermute(pick(total, col ^ d, 2), 'col', turns[d - 1])  13.6 us
  transfers between devices with their start and end apart: 53, of which 24 were waited for; matrix products, arithmetic and copies ran while one was open for 8% of the time, Pallas kernels for 13%

profile of v1, /device:TPU:0, one launch (start us, length us, event | category | flops | bytes accessed | tf_op | source)
XLA Modules:
  0.0 286.4 jit_solution(17728494415856520645)
XLA Ops:
  0.7 2.8 copy-done
  3.5 9.6 %shard_map.77 = (bf16[3,2,512,384]{3,2,1,0:T(8,128)(2,1)S(1)}, bf16[4,2,512,384]{3,2,1,0:T(8,128)(2,1)S(1)}) custom-call(s32[3]{0:T(128)S(1)} %pad_add_fusion.meta_ref, bf16[4,4,512,1024]{3,2,1,0:T(8,128)(2,1)} %bitcast.149, bf16[4,1024,768]{2,1,0:T(8,128)(2,1)S(1)} %copy-done), custom_call_target="tpu_custom_call" | custom-call | flops 3221225472 | bytes 13107200 | tf_op jit(solution)/shard_map/pallas_call | solution.py:57
  13.6 9.6 %shard_map.79 = (bf16[3,2,512,384]{3,2,1,0:T(8,128)(2,1)S(1)}, bf16[4,2,512,384]{3,2,1,0:T(8,128)(2,1)S(1)}) custom-call(s32[3]{0:T(128)S(1)} %pad_add_fusion.meta_ref, bf16[4,4,512,1024]{3,2,1,0:T(8,128)(2,1)} %bitcast.150, bf16[4,1024,768]{2,1,0:T(8,128)(2,1)S(1)} %copy-done), custom_call_target="tpu_custom_call" | custom-call | flops 3221225472 | bytes 13107200 | tf_op jit(solution)/shard_map/pallas_call | solution.py:57
  23.6 5.0 %collective-permute-start.1 = (bf16[2,512,384]{2,1,0:T(8,128)(2,1)S(1)}, bf16[2,512,384]{2,1,0:T(8,128)(2,1)S(1)}, u32[]{:S(2)}, u32[]{:S(2)}) collective-permute-start(bf16[2,512,384]{2,1,0:T(8,128)(2,1)S(1)} %fusion.14), channel_id=1, source_target_pairs={{0,8},{28,20},{1,9},{29,21},{2,10},{30,22},{3,11},{31,23}} | collective-permute-start | bytes 2359304 | tf_op jit(solution)/shard_map/ppermute | solution.py:154
  28.8 3.9 %collective-permute-start.14 = (bf16[2,512,384]{2,1,0:T(8,128)(2,1)S(1)}, bf16[2,512,384]{2,1,0:T(8,128)(2,1)S(1)}, u32[]{:S(2)}, u32[]{:S(2)}) collective-permute-start(bf16[2,512,384]{2,1,0:T(8,128)(2,1)S(1)} %fusion.16), channel_id=1, source_target_pairs={{0,8},{28,20},{1,9},{29,21},{2,10},{30,22},{3,11},{31,23}} | collective-permute-start | bytes 2359304 | tf_op jit(solution)/shard_map/ppermute | solution.py:154
  32.7 5.3 %collective-permute-done.1 = bf16[2,512,384]{2,1,0:T(8,128)(2,1)S(1)} collective-permute-done((bf16[2,512,384]{2,1,0:T(8,128)(2,1)S(1)}, bf16[2,512,384]{2,1,0:T(8,128)(2,1)S(1)}, u32[]{:S(2)}, u32[]{:S(2)}) %collective-permute-start.1) | collective-permute-done | bytes 786464 | tf_op jit(solution)/shard_map/ppermute | solution.py:154
  38.3 4.4 %collective-permute-start.2 = (bf16[2,512,384]{2,1,0:T(8,128)(2,1)S(1)}, bf16[2,512,384]{2,1,0:T(8,128)(2,1)S(1)}, u32[]{:S(2)}, u32[]{:S(2)}) collective-permute-start(bf16[2,512,384]{2,1,0:T(8,128)(2,1)S(1)} %fusion.10), channel_id=1, source_target_pairs={{0,8},{8,16},{28,20},{20,12},{1,9},{9,17},{29,21},{21,13},{2,10},{... | collective-permute-start | bytes 2359304 | tf_op jit(solution)/shard_map/ppermute | solution.py:154
  42.8 3.7 %collective-permute-done.14 = bf16[2,512,384]{2,1,0:T(8,128)(2,1)S(1)} collective-permute-done((bf16[2,512,384]{2,1,0:T(8,128)(2,1)S(1)}, bf16[2,512,384]{2,1,0:T(8,128)(2,1)S(1)}, u32[]{:S(2)}, u32[]{:S(2)}) %collective-permute-start.14) | collective-permute-done | bytes 786464 | tf_op jit(solution)/shard_map/ppermute | solution.py:154
  46.7 4.4 %collective-permute-start.15 = (bf16[2,512,384]{2,1,0:T(8,128)(2,1)S(1)}, bf16[2,512,384]{2,1,0:T(8,128)(2,1)S(1)}, u32[]{:S(2)}, u32[]{:S(2)}) collective-permute-start(bf16[2,512,384]{2,1,0:T(8,128)(2,1)S(1)} %fusion.6), channel_id=1, source_target_pairs={{0,8},{8,16},{28,20},{20,12},{1,9},{9,17},{29,21},{21,13},{2,10},{... | collective-permute-start | bytes 2359304 | tf_op jit(solution)/shard_map/ppermute | solution.py:154
  51.2 9.6 %shard_map.78 = (bf16[3,2,512,384]{3,2,1,0:T(8,128)(2,1)S(1)}, bf16[4,2,512,384]{3,2,1,0:T(8,128)(2,1)S(1)}) custom-call(s32[3]{0:T(128)S(1)} %pad_add_fusion.meta_ref, bf16[4,4,512,1024]{3,2,1,0:T(8,128)(2,1)} %bitcast.151, bf16[4,1024,768]{2,1,0:T(8,128)(2,1)S(1)} %copy-done), custom_call_target="tpu_custom_call" | custom-call | flops 3221225472 | bytes 13107200 | tf_op jit(solution)/shard_map/pallas_call | solution.py:57
  61.2 1.9 collective-permute-start.3
  63.6 4.4 %collective-permute-start.16 = (bf16[2,512,384]{2,1,0:T(8,128)(2,1)S(1)}, bf16[2,512,384]{2,1,0:T(8,128)(2,1)S(1)}, u32[]{:S(2)}, u32[]{:S(2)}) collective-permute-start(bf16[2,512,384]{2,1,0:T(8,128)(2,1)S(1)} %fusion.7), channel_id=1, source_target_pairs={{0,8},{8,16},{16,24},{28,20},{20,12},{12,4},{1,9},{9,17},{17,25},{... | collective-permute-start | bytes 2359304 | tf_op jit(solution)/shard_map/ppermute | solution.py:154
  68.0 9.6 %shard_map.81 = (bf16[3,2,512,384]{3,2,1,0:T(8,128)(2,1)S(1)}, bf16[4,2,512,384]{3,2,1,0:T(8,128)(2,1)S(1)}) custom-call(s32[3]{0:T(128)S(1)} %pad_add_fusion.meta_ref, bf16[4,4,512,1024]{3,2,1,0:T(8,128)(2,1)} %bitcast.152, bf16[4,1024,768]{2,1,0:T(8,128)(2,1)S(1)} %copy-done), custom_call_target="tpu_custom_call" | custom-call | flops 3221225472 | bytes 13107200 | tf_op jit(solution)/shard_map/pallas_call | solution.py:57
  78.5 2.5 collective-permute-done.16
  81.2 1.9 collective-permute-start.17
  83.6 2.4 collective-permute-start.6
  86.3 3.4 %collective-permute-start.18 = (bf16[2,512,384]{2,1,0:T(8,128)(2,1)S(1)}, bf16[2,512,384]{2,1,0:T(8,128)(2,1)S(1)}, u32[]{:S(2)}, u32[]{:S(2)}) collective-permute-start(bf16[2,512,384]{2,1,0:T(8,128)(2,1)S(1)} %add_convert_fusion.3.refs_4_), channel_id=1, source_target_pairs={{0,8},{8,16},{16,24},{28,20},{20,12},{12,4},{1,9},{9,17},{17,25},{... | collective-permute-start | bytes 2359304 | tf_op jit(solution)/shard_map/ppermute | solution.py:154
  89.9 5.5 %collective-permute-done.6.refs_1_ = bf16[2,512,384]{2,1,0:T(8,128)(2,1)S(1)} collective-permute-done((bf16[2,512,384]{2,1,0:T(8,128)(2,1)S(1)}, bf16[2,512,384]{2,1,0:T(8,128)(2,1)S(1)}, u32[]{:S(2)}, u32[]{:S(2)}) %collective-permute-start.6) | collective-permute-done | bytes 786464 | tf_op jit(solution)/shard_map/ppermute | solution.py:154
  95.4 4.4 %collective-permute-start.7 = (bf16[2,512,384]{2,1,0:T(8,128)(2,1)S(1)}, bf16[2,512,384]{2,1,0:T(8,128)(2,1)S(1)}, u32[]{:S(2)}, u32[]{:S(2)}) collective-permute-start(bf16[2,512,384]{2,1,0:T(8,128)(2,1)S(1)} %fusion.15), channel_id=1, source_target_pairs={{0,8},{28,20},{1,9},{29,21},{2,10},{30,22},{3,11},{31,23}} | collective-permute-start | bytes 2359304 | tf_op jit(solution)/shard_map/ppermute | solution.py:154
  100.1 3.8 %collective-permute-done.18.refs_5_ = bf16[2,512,384]{2,1,0:T(8,128)(2,1)S(1)} collective-permute-done((bf16[2,512,384]{2,1,0:T(8,128)(2,1)S(1)}, bf16[2,512,384]{2,1,0:T(8,128)(2,1)S(1)}, u32[]{:S(2)}, u32[]{:S(2)}) %collective-permute-start.18) | collective-permute-done | bytes 786464 | tf_op jit(solution)/shard_map/ppermute | solution.py:154
  103.8 4.4 %collective-permute-start.23 = (bf16[2,512,384]{2,1,0:T(8,128)(2,1)S(1)}, bf16[2,512,384]{2,1,0:T(8,128)(2,1)S(1)}, u32[]{:S(2)}, u32[]{:S(2)}) collective-permute-start(bf16[2,512,384]{2,1,0:T(8,128)(2,1)S(1)} %fusion.17), channel_id=1, source_target_pairs={{0,8},{28,20},{1,9},{29,21},{2,10},{30,22},{3,11},{31,23}} | collective-permute-start | bytes 2359304 | tf_op jit(solution)/shard_map/ppermute | solution.py:154
  108.3 1.6 collective-permute-start.11
  109.8 1.6 collective-permute-start.19
  112.6 4.4 %collective-permute-start.8 = (bf16[2,512,384]{2,1,0:T(8,128)(2,1)S(1)}, bf16[2,512,384]{2,1,0:T(8,128)(2,1)S(1)}, u32[]{:S(2)}, u32[]{:S(2)}) collective-permute-start(bf16[2,512,384]{2,1,0:T(8,128)(2,1)S(1)} %fusion.8), channel_id=1, source_target_pairs={{0,8},{8,16},{28,20},{20,12},{1,9},{9,17},{29,21},{21,13},{2,10},{... | collective-permute-start | bytes 2359304 | tf_op jit(solution)/shard_map/ppermute | solution.py:154
  117.0 3.7 %collective-permute-done.23 = bf16[2,512,384]{2,1,0:T(8,128)(2,1)S(1)} collective-permute-done((bf16[2,512,384]{2,1,0:T(8,128)(2,1)S(1)}, bf16[2,512,384]{2,1,0:T(8,128)(2,1)S(1)}, u32[]{:S(2)}, u32[]{:S(2)}) %collective-permute-start.23) | collective-permute-done | bytes 786464 | tf_op jit(solution)/shard_map/ppermute | solution.py:154
  121.0 4.4 %collective-permute-start.24 = (bf16[2,512,384]{2,1,0:T(8,128)(2,1)S(1)}, bf16[2,512,384]{2,1,0:T(8,128)(2,1)S(1)}, u32[]{:S(2)}, u32[]{:S(2)}) collective-permute-start(bf16[2,512,384]{2,1,0:T(8,128)(2,1)S(1)} %fusion.4), channel_id=1, source_target_pairs={{0,8},{8,16},{28,20},{20,12},{1,9},{9,17},{29,21},{21,13},{2,10},{... | collective-permute-start | bytes 2359304 | tf_op jit(solution)/shard_map/ppermute | solution.py:154
  125.4 1.6 collective-permute-start.12
  127.0 1.6 collective-permute-start.20
  130.3 9.9 %collective-permute-start.9 = (bf16[2,512,384]{2,1,0:T(8,128)(2,1)}, bf16[2,512,384]{2,1,0:T(8,128)(2,1)}, u32[]{:S(2)}, u32[]{:S(2)}) collective-permute-start(bf16[2,512,384]{2,1,0:T(8,128)(2,1)} %fusion.9), channel_id=1, source_target_pairs={{0,8},{8,16},{16,24},{28,20},{20,12},{12,4},{1,9},{9,17},{17,25},{... | collective-permute-start | bytes 2359304 | tf_op jit(solution)/shard_map/ppermute | solution.py:154
  141.4 7.0 %collective-permute-start.25 = (bf16[2,512,384]{2,1,0:T(8,128)(2,1)}, bf16[2,512,384]{2,1,0:T(8,128)(2,1)}, u32[]{:S(2)}, u32[]{:S(2)}) collective-permute-start(bf16[2,512,384]{2,1,0:T(8,128)(2,1)} %fusion.5), channel_id=1, source_target_pairs={{0,8},{8,16},{16,24},{28,20},{20,12},{12,4},{1,9},{9,17},{17,25},{... | collective-permute-start | bytes 2359304 | tf_op jit(solution)/shard_map/ppermute | solution.py:154
  148.7 8.9 %shard_map.80 = bf16[56,32,384]{2,1,0:T(8,128)(2,1)} custom-call(s32[56]{0:T(128)S(1)} %reshape.89.table_ref, s32[3]{0:T(128)S(1)} %pad_add_fusion.meta_ref, bf16[4,224,2048]{2,1,0:T(8,128)(2,1)} %mine_ref.3, bf16[4,224,2048]{2,1,0:T(8,128)(2,1)} %collective-permute-done.10.theirs_ref, bf16[2,512,384]{2,1,0:T(8,128)(2,1)S(1)} %add_convert_fusion.6.refs_0_, ...), custom_call_target="tpu_custom_call" | custom-call | flops 2818572288 | bytes 8716288 | tf_op jit(solution)/shard_map/pallas_call | solution.py:122
  157.6 2.5 fusion.2
  160.1 2.6 fusion
  164.1 1.6 add_convert_fusion.2.refs_0_
  165.7 4.8 %collective-permute-start.37 = (bf16[2,512,384]{2,1,0:T(8,128)(2,1)S(1)}, bf16[2,512,384]{2,1,0:T(8,128)(2,1)}, u32[]{:S(2)}, u32[]{:S(2)}) collective-permute-start(bf16[2,512,384]{2,1,0:T(8,128)(2,1)S(1)} %add_convert_fusion.2.refs_0_), channel_id=1, source_target_pairs={{0,8},{8,16},{16,24},{28,20},{20,12},{12,4},{1,9},{9,17},{17,25},{... | collective-permute-start | bytes 2359304 | tf_op jit(solution)/shard_map/ppermute | solution.py:154
  170.4 1.6 add_convert_fusion.refs_4_
  172.0 3.8 %collective-permute-start.40 = (bf16[2,512,384]{2,1,0:T(8,128)(2,1)S(1)}, bf16[2,512,384]{2,1,0:T(8,128)(2,1)}, u32[]{:S(2)}, u32[]{:S(2)}) collective-permute-start(bf16[2,512,384]{2,1,0:T(8,128)(2,1)S(1)} %add_convert_fusion.refs_4_), channel_id=1, source_target_pairs={{0,8},{8,16},{16,24},{28,20},{20,12},{12,4},{1,9},{9,17},{17,25},{... | collective-permute-start | bytes 2359304 | tf_op jit(solution)/shard_map/ppermute | solution.py:154
  175.8 1.3 fusion.13
  178.7 1.5 collective-permute-start.28
  180.2 1.5 collective-permute-start.30
  182.2 2.1 collective-permute-done.28
  184.4 2.9 %collective-permute-done.30 = bf16[4,7,8,384]{3,2,1,0:T(8,128)(2,1)S(1)} collective-permute-done((bf16[4,7,8,384]{3,2,1,0:T(8,128)(2,1)}, bf16[4,7,8,384]{3,2,1,0:T(8,128)(2,1)S(1)}, u32[]{:S(2)}, u32[]{:S(2)}) %collective-permute-start.30) | collective-permute-done | bytes 172064 | tf_op jit(solution)/shard_map/ppermute | solution.py:177
  190.3 1.6 collective-permute-start.38
  191.9 1.5 collective-permute-start.41
  194.1 4.7 %collective-permute-start.31 = (bf16[7,8,384]{2,1,0:T(8,128)(2,1)}, bf16[7,8,384]{2,1,0:T(8,128)(2,1)S(1)}, u32[]{:S(2)}, u32[]{:S(2)}) collective-permute-start(bf16[7,8,384]{2,1,0:T(8,128)(2,1)} %get-tuple-element.49), channel_id=1, source_target_pairs={{0,8},{4,12},{8,16},{12,20},{16,24},{20,28},{24,0},{28,4},{1,9},{5... | collective-permute-start | bytes 129032 | tf_op jit(solution)/shard_map/ppermute | solution.py:183
  198.7 1.5 collective-permute-start.32
  200.7 3.0 %collective-permute-done.33 = bf16[7,8,384]{2,1,0:T(8,128)(2,1)S(1)} collective-permute-done((bf16[7,8,384]{2,1,0:T(8,128)(2,1)}, bf16[7,8,384]{2,1,0:T(8,128)(2,1)S(1)}, u32[]{:S(2)}, u32[]{:S(2)}) %collective-permute-start.33) | collective-permute-done | bytes 43040 | tf_op jit(solution)/shard_map/ppermute | solution.py:183
  205.9 1.7 collective-permute-start.39
  207.5 1.6 collective-permute-start.42
  209.2 9.4 %shard_map.82 = bf16[56,32,384]{2,1,0:T(8,128)(2,1)} custom-call(s32[56]{0:T(128)S(1)} %reshape.89.table_ref, s32[3]{0:T(128)S(1)} %pad_add_fusion.meta_ref, bf16[4,224,2048]{2,1,0:T(8,128)(2,1)} %mine_ref.3, bf16[4,224,2048]{2,1,0:T(8,128)(2,1)} %collective-permute-done.10.theirs_ref, bf16[2,512,384]{2,1,0:T(8,128)(2,1)S(1)} %add_convert_fusion.2.refs_0_, ...), custom_call_target="tpu_custom_call" | custom-call | flops 2818572288 | bytes 8716288 | tf_op jit(solution)/shard_map/pallas_call | solution.py:122
  219.9 25.2 %collective-permute-start.43 = (bf16[4,7,4,8,384]{4,3,2,1,0:T(8,128)(2,1)S(1)}, bf16[4,7,4,8,384]{4,3,2,1,0:T(8,128)(2,1)S(1)}, u32[]{:S(2)}, u32[]{:S(2)}) collective-permute-start(bf16[4,7,4,8,384]{4,3,2,1,0:T(8,128)(2,1)S(1)} %dynamic-slice_bitcast_fusion), channel_id=1, source_target_pairs={{0,4},{4,0},{8,12},{12,8},{16,20},{20,16},{24,28},{28,24},{1,5},{5... | collective-permute-start | bytes 2064392 | tf_op jit(solution)/shard_map/ppermute | solution.py:172
  245.1 1.5 collective-permute-start.34
  247.3 1.5 collective-permute-start.35
  249.3 2.0 collective-permute-done.35
  251.6 1.5 collective-permute-start.44
  253.1 1.5 collective-permute-start.46
  255.2 3.6 %collective-permute-done.44 = bf16[4,7,8,384]{3,2,1,0:T(8,128)(2,1)S(1)} collective-permute-done((bf16[4,7,8,384]{3,2,1,0:T(8,128)(2,1)S(1)}, bf16[4,7,8,384]{3,2,1,0:T(8,128)(2,1)S(1)}, u32[]{:S(2)}, u32[]{:S(2)}) %collective-permute-start.44) | collective-permute-done | bytes 172064 | tf_op jit(solution)/shard_map/ppermute | solution.py:177
  258.8 2.4 collective-permute-done.46
  261.3 1.4 collective-permute-done.45
  262.8 9.8 %collective-permute-start.49 = (bf16[7,8,384]{2,1,0:T(8,128)(2,1)S(1)}, bf16[7,8,384]{2,1,0:T(8,128)(2,1)S(1)}, u32[]{:S(2)}, u32[]{:S(2)}) collective-permute-start(bf16[7,8,384]{2,1,0:T(8,128)(2,1)S(1)} %get-tuple-element.47), channel_id=1, source_target_pairs={{0,24},{4,28},{8,0},{12,4},{16,8},{20,12},{24,16},{28,20},{1,25},{... | collective-permute-start | bytes 129032 | tf_op jit(solution)/shard_map/ppermute | solution.py:183
  273.1 1.4 collective-permute-done.47
  274.5 3.0 %collective-permute-done.48 = bf16[7,8,384]{2,1,0:T(8,128)(2,1)S(1)} collective-permute-done((bf16[7,8,384]{2,1,0:T(8,128)(2,1)S(1)}, bf16[7,8,384]{2,1,0:T(8,128)(2,1)S(1)}, u32[]{:S(2)}, u32[]{:S(2)}) %collective-permute-start.48) | collective-permute-done | bytes 43040 | tf_op jit(solution)/shard_map/ppermute | solution.py:183
  280.5 1.9 collective-permute-start.52
  283.6 1.9 collective-permute-done.52
  (128 shorter events, 28.8 us)
Async XLA Ops:
  0.7 2.8 copy-start
  13.1 10.3 %collective-permute-start = (bf16[3,2,512,384]{3,2,1,0:T(8,128)(2,1)S(1)}, bf16[3,2,512,384]{3,2,1,0:T(8,128)(2,1)S(1)}, u32[]{:S(2)}, u32[]{:S(2)}) collective-permute-start(bf16[3,2,512,384]{3,2,1,0:T(8,128)(2,1)S(1)} %get-tuple-element.20), channel_id=1, source_target_pairs={{0,4},{4,0},{8,12},{12,8},{16,20},{20,16},{24,28},{28,24},{1,5},{5... | collective-permute-start | bytes 7077896 | tf_op jit(solution)/shard_map/ppermute | solution.py:164
  23.2 5.3 %collective-permute-start.13 = (bf16[3,2,512,384]{3,2,1,0:T(8,128)(2,1)S(1)}, bf16[3,2,512,384]{3,2,1,0:T(8,128)(2,1)S(1)}, u32[]{:S(2)}, u32[]{:S(2)}) collective-permute-start(bf16[3,2,512,384]{3,2,1,0:T(8,128)(2,1)S(1)} %get-tuple-element.28), channel_id=1, source_target_pairs={{0,4},{4,0},{8,12},{12,8},{16,20},{20,16},{24,28},{28,24},{1,5},{5... | collective-permute-start | bytes 7077896 | tf_op jit(solution)/shard_map/ppermute | solution.py:164
  23.6 14.4 %collective-permute-start.1 = (bf16[2,512,384]{2,1,0:T(8,128)(2,1)S(1)}, bf16[2,512,384]{2,1,0:T(8,128)(2,1)S(1)}, u32[]{:S(2)}, u32[]{:S(2)}) collective-permute-start(bf16[2,512,384]{2,1,0:T(8,128)(2,1)S(1)} %fusion.14), channel_id=1, source_target_pairs={{0,8},{28,20},{1,9},{29,21},{2,10},{30,22},{3,11},{31,23}} | collective-permute-start | bytes 2359304 | tf_op jit(solution)/shard_map/ppermute | solution.py:154
  28.8 17.6 %collective-permute-start.14 = (bf16[2,512,384]{2,1,0:T(8,128)(2,1)S(1)}, bf16[2,512,384]{2,1,0:T(8,128)(2,1)S(1)}, u32[]{:S(2)}, u32[]{:S(2)}) collective-permute-start(bf16[2,512,384]{2,1,0:T(8,128)(2,1)S(1)} %fusion.16), channel_id=1, source_target_pairs={{0,8},{28,20},{1,9},{29,21},{2,10},{30,22},{3,11},{31,23}} | collective-permute-start | bytes 2359304 | tf_op jit(solution)/shard_map/ppermute | solution.py:154
  38.3 22.5 %collective-permute-start.2 = (bf16[2,512,384]{2,1,0:T(8,128)(2,1)S(1)}, bf16[2,512,384]{2,1,0:T(8,128)(2,1)S(1)}, u32[]{:S(2)}, u32[]{:S(2)}) collective-permute-start(bf16[2,512,384]{2,1,0:T(8,128)(2,1)S(1)} %fusion.10), channel_id=1, source_target_pairs={{0,8},{8,16},{28,20},{20,12},{1,9},{9,17},{29,21},{21,13},{2,10},{... | collective-permute-start | bytes 2359304 | tf_op jit(solution)/shard_map/ppermute | solution.py:154
  46.7 16.5 %collective-permute-start.15 = (bf16[2,512,384]{2,1,0:T(8,128)(2,1)S(1)}, bf16[2,512,384]{2,1,0:T(8,128)(2,1)S(1)}, u32[]{:S(2)}, u32[]{:S(2)}) collective-permute-start(bf16[2,512,384]{2,1,0:T(8,128)(2,1)S(1)} %fusion.6), channel_id=1, source_target_pairs={{0,8},{8,16},{28,20},{20,12},{1,9},{9,17},{29,21},{21,13},{2,10},{... | collective-permute-start | bytes 2359304 | tf_op jit(solution)/shard_map/ppermute | solution.py:154
  60.8 68.3 %copy-start.1 = (bf16[4,2,512,384]{3,2,1,0:T(8,128)(2,1)}, bf16[4,2,512,384]{3,2,1,0:T(8,128)(2,1)S(1)}, u32[]{:S(2)}) copy-start(bf16[4,2,512,384]{3,2,1,0:T(8,128)(2,1)S(1)} %get-tuple-element.22) | copy-start | bytes 9437188
  60.8 28.8 %collective-permute-start.5 = (bf16[3,2,512,384]{3,2,1,0:T(8,128)(2,1)S(1)}, bf16[3,2,512,384]{3,2,1,0:T(8,128)(2,1)S(1)}, u32[]{:S(2)}, u32[]{:S(2)}) collective-permute-start(bf16[3,2,512,384]{3,2,1,0:T(8,128)(2,1)S(1)} %get-tuple-element.23), channel_id=1, source_target_pairs={{0,4},{4,0},{8,12},{12,8},{16,20},{20,16},{24,28},{28,24},{1,5},{5... | collective-permute-start | bytes 7077896 | tf_op jit(solution)/shard_map/ppermute | solution.py:164
  61.2 16.5 %collective-permute-start.3 = (bf16[2,512,384]{2,1,0:T(8,128)(2,1)S(1)}, bf16[2,512,384]{2,1,0:T(8,128)(2,1)S(1)}, u32[]{:S(2)}, u32[]{:S(2)}) collective-permute-start(bf16[2,512,384]{2,1,0:T(8,128)(2,1)S(1)} %fusion.11), channel_id=1, source_target_pairs={{0,8},{8,16},{16,24},{28,20},{20,12},{12,4},{1,9},{9,17},{17,25},{... | collective-permute-start | bytes 2359304 | tf_op jit(solution)/shard_map/ppermute | solution.py:154
  63.6 17.4 %collective-permute-start.16 = (bf16[2,512,384]{2,1,0:T(8,128)(2,1)S(1)}, bf16[2,512,384]{2,1,0:T(8,128)(2,1)S(1)}, u32[]{:S(2)}, u32[]{:S(2)}) collective-permute-start(bf16[2,512,384]{2,1,0:T(8,128)(2,1)S(1)} %fusion.7), channel_id=1, source_target_pairs={{0,8},{8,16},{16,24},{28,20},{20,12},{12,4},{1,9},{9,17},{17,25},{... | collective-permute-start | bytes 2359304 | tf_op jit(solution)/shard_map/ppermute | solution.py:154
  77.6 62.6 %copy-start.2 = (bf16[4,2,512,384]{3,2,1,0:T(8,128)(2,1)}, bf16[4,2,512,384]{3,2,1,0:T(8,128)(2,1)S(1)}, u32[]{:S(2)}) copy-start(bf16[4,2,512,384]{3,2,1,0:T(8,128)(2,1)S(1)} %get-tuple-element.31) | copy-start | bytes 9437188
  77.6 22.2 %collective-permute-start.22 = (bf16[3,2,512,384]{3,2,1,0:T(8,128)(2,1)S(1)}, bf16[3,2,512,384]{3,2,1,0:T(8,128)(2,1)S(1)}, u32[]{:S(2)}, u32[]{:S(2)}) collective-permute-start(bf16[3,2,512,384]{3,2,1,0:T(8,128)(2,1)S(1)} %get-tuple-element.32), channel_id=1, source_target_pairs={{0,4},{4,0},{8,12},{12,8},{16,20},{20,16},{24,28},{28,24},{1,5},{5... | collective-permute-start | bytes 7077896 | tf_op jit(solution)/shard_map/ppermute | solution.py:164
  78.0 5.4 %collective-permute-start.4 = (bf16[2,512,384]{2,1,0:T(8,128)(2,1)S(1)}, bf16[2,512,384]{2,1,0:T(8,128)(2,1)S(1)}, u32[]{:S(2)}, u32[]{:S(2)}) collective-permute-start(bf16[2,512,384]{2,1,0:T(8,128)(2,1)S(1)} %fusion.3), channel_id=1, source_target_pairs={{0,4},{4,0},{8,12},{12,8},{16,20},{20,16},{24,28},{28,24},{1,5},{5... | collective-permute-start | bytes 2359304 | tf_op jit(solution)/shard_map/ppermute | solution.py:228
  81.2 4.8 %collective-permute-start.17 = (bf16[2,512,384]{2,1,0:T(8,128)(2,1)S(1)}, bf16[2,512,384]{2,1,0:T(8,128)(2,1)S(1)}, u32[]{:S(2)}, u32[]{:S(2)}) collective-permute-start(bf16[2,512,384]{2,1,0:T(8,128)(2,1)S(1)} %fusion.1), channel_id=1, source_target_pairs={{0,4},{4,0},{8,12},{12,8},{16,20},{20,16},{24,28},{28,24},{1,5},{5... | collective-permute-start | bytes 2359304 | tf_op jit(solution)/shard_map/ppermute | solution.py:228
  83.6 11.8 %collective-permute-start.6 = (bf16[2,512,384]{2,1,0:T(8,128)(2,1)S(1)}, bf16[2,512,384]{2,1,0:T(8,128)(2,1)S(1)}, u32[]{:S(2)}, u32[]{:S(2)}) collective-permute-start(bf16[2,512,384]{2,1,0:T(8,128)(2,1)S(1)} %add_convert_fusion.6.refs_0_), channel_id=1, source_target_pairs={{0,8},{8,16},{16,24},{28,20},{20,12},{12,4},{1,9},{9,17},{17,25},{... | collective-permute-start | bytes 2359304 | tf_op jit(solution)/shard_map/ppermute | solution.py:154
  86.0 62.7 %collective-permute-start.10 = (bf16[4,224,2048]{2,1,0:T(8,128)(2,1)}, bf16[4,224,2048]{2,1,0:T(8,128)(2,1)}, u32[]{:S(2)}, u32[]{:S(2)}) collective-permute-start(bf16[4,224,2048]{2,1,0:T(8,128)(2,1)} %mine_ref.3), channel_id=1, source_target_pairs={{0,4},{4,0},{8,12},{12,8},{16,20},{20,16},{24,28},{28,24},{1,5},{5... | collective-permute-start | bytes 11010056 | tf_op jit(solution)/shard_map/ppermute | solution.py:219
  86.3 17.6 %collective-permute-start.18 = (bf16[2,512,384]{2,1,0:T(8,128)(2,1)S(1)}, bf16[2,512,384]{2,1,0:T(8,128)(2,1)S(1)}, u32[]{:S(2)}, u32[]{:S(2)}) collective-permute-start(bf16[2,512,384]{2,1,0:T(8,128)(2,1)S(1)} %add_convert_fusion.3.refs_4_), channel_id=1, source_target_pairs={{0,8},{8,16},{16,24},{28,20},{20,12},{12,4},{1,9},{9,17},{17,25},{... | collective-permute-start | bytes 2359304 | tf_op jit(solution)/shard_map/ppermute | solution.py:154
  95.4 16.9 %collective-permute-start.7 = (bf16[2,512,384]{2,1,0:T(8,128)(2,1)S(1)}, bf16[2,512,384]{2,1,0:T(8,128)(2,1)S(1)}, u32[]{:S(2)}, u32[]{:S(2)}) collective-permute-start(bf16[2,512,384]{2,1,0:T(8,128)(2,1)S(1)} %fusion.15), channel_id=1, source_target_pairs={{0,8},{28,20},{1,9},{29,21},{2,10},{30,22},{3,11},{31,23}} | collective-permute-start | bytes 2359304 | tf_op jit(solution)/shard_map/ppermute | solution.py:154
  103.8 16.9 %collective-permute-start.23 = (bf16[2,512,384]{2,1,0:T(8,128)(2,1)S(1)}, bf16[2,512,384]{2,1,0:T(8,128)(2,1)S(1)}, u32[]{:S(2)}, u32[]{:S(2)}) collective-permute-start(bf16[2,512,384]{2,1,0:T(8,128)(2,1)S(1)} %fusion.17), channel_id=1, source_target_pairs={{0,8},{28,20},{1,9},{29,21},{2,10},{30,22},{3,11},{31,23}} | collective-permute-start | bytes 2359304 | tf_op jit(solution)/shard_map/ppermute | solution.py:154
  108.3 17.2 %collective-permute-start.11 = (bf16[2,512,384]{2,1,0:T(8,128)(2,1)S(1)}, bf16[2,512,384]{2,1,0:T(8,128)(2,1)}, u32[]{:S(2)}, u32[]{:S(2)}) collective-permute-start(bf16[2,512,384]{2,1,0:T(8,128)(2,1)S(1)} %collective-permute-done.6.refs_1_), channel_id=1, source_target_pairs={{8,16},{16,24},{20,12},{12,4},{9,17},{17,25},{21,13},{13,5},{10,18... | collective-permute-start | bytes 2359304 | tf_op jit(solution)/shard_map/ppermute | solution.py:154
  109.8 17.2 %collective-permute-start.19 = (bf16[2,512,384]{2,1,0:T(8,128)(2,1)S(1)}, bf16[2,512,384]{2,1,0:T(8,128)(2,1)}, u32[]{:S(2)}, u32[]{:S(2)}) collective-permute-start(bf16[2,512,384]{2,1,0:T(8,128)(2,1)S(1)} %collective-permute-done.18.refs_5_), channel_id=1, source_target_pairs={{8,16},{16,24},{20,12},{12,4},{9,17},{17,25},{21,13},{13,5},{10,18... | collective-permute-start | bytes 2359304 | tf_op jit(solution)/shard_map/ppermute | solution.py:154
  112.6 16.5 %collective-permute-start.8 = (bf16[2,512,384]{2,1,0:T(8,128)(2,1)S(1)}, bf16[2,512,384]{2,1,0:T(8,128)(2,1)S(1)}, u32[]{:S(2)}, u32[]{:S(2)}) collective-permute-start(bf16[2,512,384]{2,1,0:T(8,128)(2,1)S(1)} %fusion.8), channel_id=1, source_target_pairs={{0,8},{8,16},{28,20},{20,12},{1,9},{9,17},{29,21},{21,13},{2,10},{... | collective-permute-start | bytes 2359304 | tf_op jit(solution)/shard_map/ppermute | solution.py:154
  121.0 19.2 %collective-permute-start.24 = (bf16[2,512,384]{2,1,0:T(8,128)(2,1)S(1)}, bf16[2,512,384]{2,1,0:T(8,128)(2,1)S(1)}, u32[]{:S(2)}, u32[]{:S(2)}) collective-permute-start(bf16[2,512,384]{2,1,0:T(8,128)(2,1)S(1)} %fusion.4), channel_id=1, source_target_pairs={{0,8},{8,16},{28,20},{20,12},{1,9},{9,17},{29,21},{21,13},{2,10},{... | collective-permute-start | bytes 2359304 | tf_op jit(solution)/shard_map/ppermute | solution.py:154
  125.4 23.2 %collective-permute-start.12 = (bf16[2,512,384]{2,1,0:T(8,128)(2,1)}, bf16[2,512,384]{2,1,0:T(8,128)(2,1)}, u32[]{:S(2)}, u32[]{:S(2)}) collective-permute-start(bf16[2,512,384]{2,1,0:T(8,128)(2,1)} %collective-permute-done.11.refs_2_), channel_id=1, source_target_pairs={{16,24},{12,4},{17,25},{13,5},{18,26},{14,6},{19,27},{15,7}} | collective-permute-start | bytes 2359304 | tf_op jit(solution)/shard_map/ppermute | solution.py:154
  127.0 21.7 %collective-permute-start.20 = (bf16[2,512,384]{2,1,0:T(8,128)(2,1)}, bf16[2,512,384]{2,1,0:T(8,128)(2,1)}, u32[]{:S(2)}, u32[]{:S(2)}) collective-permute-start(bf16[2,512,384]{2,1,0:T(8,128)(2,1)} %collective-permute-done.19.refs_6_), channel_id=1, source_target_pairs={{16,24},{12,4},{17,25},{13,5},{18,26},{14,6},{19,27},{15,7}} | collective-permute-start | bytes 2359304 | tf_op jit(solution)/shard_map/ppermute | solution.py:154
  130.3 18.1 %copy-start.12 = (s32[56,4]{0,1:T(4,128)S(1)}, s32[56,4]{0,1:T(4,128)}, u32[]{:S(2)}) copy-start(s32[56,4]{0,1:T(4,128)} %param.11) | copy-start | bytes 2692
  130.3 18.1 %copy-start.13 = (s32[56,4,1]{0,2,1:T(1,128)S(1)}, s32[56,4,1]{0,2,1:T(1,128)}, u32[]{:S(2)}) copy-start(s32[56,4,1]{0,2,1:T(1,128)} %param.10) | copy-start | bytes 2692
  130.3 27.3 %collective-permute-start.9 = (bf16[2,512,384]{2,1,0:T(8,128)(2,1)}, bf16[2,512,384]{2,1,0:T(8,128)(2,1)}, u32[]{:S(2)}, u32[]{:S(2)}) collective-permute-start(bf16[2,512,384]{2,1,0:T(8,128)(2,1)} %fusion.9), channel_id=1, source_target_pairs={{0,8},{8,16},{16,24},{28,20},{20,12},{12,4},{1,9},{9,17},{17,25},{... | collective-permute-start | bytes 2359304 | tf_op jit(solution)/shard_map/ppermute | solution.py:154
  141.4 18.6 %collective-permute-start.25 = (bf16[2,512,384]{2,1,0:T(8,128)(2,1)}, bf16[2,512,384]{2,1,0:T(8,128)(2,1)}, u32[]{:S(2)}, u32[]{:S(2)}) collective-permute-start(bf16[2,512,384]{2,1,0:T(8,128)(2,1)} %fusion.5), channel_id=1, source_target_pairs={{0,8},{8,16},{16,24},{28,20},{20,12},{12,4},{1,9},{9,17},{17,25},{... | collective-permute-start | bytes 2359304 | tf_op jit(solution)/shard_map/ppermute | solution.py:154
  160.1 3.0 %copy-start.3 = (bf16[56,32,384]{2,1,0:T(8,128)(2,1)S(1)}, bf16[56,32,384]{2,1,0:T(8,128)(2,1)}, u32[]{:S(2)}) copy-start(bf16[56,32,384]{2,1,0:T(8,128)(2,1)} %shard_map.80) | copy-start | bytes 4128772
  160.1 4.0 %collective-permute-start.21 = (bf16[2,512,384]{2,1,0:T(8,128)(2,1)}, bf16[2,512,384]{2,1,0:T(8,128)(2,1)}, u32[]{:S(2)}, u32[]{:S(2)}) collective-permute-start(bf16[2,512,384]{2,1,0:T(8,128)(2,1)} %fusion.2), channel_id=1, source_target_pairs={{0,4},{4,0},{8,12},{12,8},{16,20},{20,16},{24,28},{28,24},{1,5},{5... | collective-permute-start | bytes 2359304 | tf_op jit(solution)/shard_map/ppermute | solution.py:228
  162.6 7.8 %collective-permute-start.26 = (bf16[2,512,384]{2,1,0:T(8,128)(2,1)}, bf16[2,512,384]{2,1,0:T(8,128)(2,1)}, u32[]{:S(2)}, u32[]{:S(2)}) collective-permute-start(bf16[2,512,384]{2,1,0:T(8,128)(2,1)} %fusion), channel_id=1, source_target_pairs={{0,4},{4,0},{8,12},{12,8},{16,20},{20,16},{24,28},{28,24},{1,5},{5... | collective-permute-start | bytes 2359304 | tf_op jit(solution)/shard_map/ppermute | solution.py:228
  164.0 11.8 %collective-permute-start.27 = (bf16[4,7,4,8,384]{4,3,2,1,0:T(8,128)(2,1)}, bf16[4,7,4,8,384]{4,3,2,1,0:T(8,128)(2,1)}, u32[]{:S(2)}, u32[]{:S(2)}) collective-permute-start(bf16[4,7,4,8,384]{4,3,2,1,0:T(8,128)(2,1)} %dynamic-slice_bitcast_fusion.1), channel_id=1, source_target_pairs={{0,4},{4,0},{8,12},{12,8},{16,20},{20,16},{24,28},{28,24},{1,5},{5... | collective-permute-start | bytes 2064392 | tf_op jit(solution)/shard_map/ppermute | solution.py:172
  165.6 10.1 %copy-start.4 = (bf16[56,32,384]{2,1,0:T(8,128)(2,1)S(1)}, bf16[56,32,384]{2,1,0:T(8,128)(2,1)}, u32[]{:S(2)}) copy-start(bf16[56,32,384]{2,1,0:T(8,128)(2,1)} %shard_map.80) | copy-start | bytes 4128772
  165.7 24.6 %collective-permute-start.37 = (bf16[2,512,384]{2,1,0:T(8,128)(2,1)S(1)}, bf16[2,512,384]{2,1,0:T(8,128)(2,1)}, u32[]{:S(2)}, u32[]{:S(2)}) collective-permute-start(bf16[2,512,384]{2,1,0:T(8,128)(2,1)S(1)} %add_convert_fusion.2.refs_0_), channel_id=1, source_target_pairs={{0,8},{8,16},{16,24},{28,20},{20,12},{12,4},{1,9},{9,17},{17,25},{... | collective-permute-start | bytes 2359304 | tf_op jit(solution)/shard_map/ppermute | solution.py:154
  172.0 19.9 %collective-permute-start.40 = (bf16[2,512,384]{2,1,0:T(8,128)(2,1)S(1)}, bf16[2,512,384]{2,1,0:T(8,128)(2,1)}, u32[]{:S(2)}, u32[]{:S(2)}) collective-permute-start(bf16[2,512,384]{2,1,0:T(8,128)(2,1)S(1)} %add_convert_fusion.refs_4_), channel_id=1, source_target_pairs={{0,8},{8,16},{16,24},{28,20},{20,12},{12,4},{1,9},{9,17},{17,25},{... | collective-permute-start | bytes 2359304 | tf_op jit(solution)/shard_map/ppermute | solution.py:154
  177.1 0.8 copy-start.6
  178.7 5.6 %collective-permute-start.28 = (bf16[4,7,8,384]{3,2,1,0:T(8,128)(2,1)}, bf16[4,7,8,384]{3,2,1,0:T(8,128)(2,1)S(1)}, u32[]{:S(2)}, u32[]{:S(2)}) collective-permute-start(bf16[4,7,8,384]{3,2,1,0:T(8,128)(2,1)} %get-tuple-element.43), channel_id=1, source_target_pairs={{0,1},{1,0},{2,3},{3,2},{4,5},{5,4},{6,7},{7,6},{8,9},{9,8},{10,11... | collective-permute-start | bytes 516104 | tf_op jit(solution)/shard_map/ppermute | solution.py:177
  180.2 7.0 %collective-permute-start.30 = (bf16[4,7,8,384]{3,2,1,0:T(8,128)(2,1)}, bf16[4,7,8,384]{3,2,1,0:T(8,128)(2,1)S(1)}, u32[]{:S(2)}, u32[]{:S(2)}) collective-permute-start(bf16[4,7,8,384]{3,2,1,0:T(8,128)(2,1)} %get-tuple-element.44), channel_id=1, source_target_pairs={{0,3},{1,2},{2,1},{3,0},{4,7},{5,6},{6,5},{7,4},{8,11},{9,10},{10,... | collective-permute-start | bytes 516104 | tf_op jit(solution)/shard_map/ppermute | solution.py:177
  181.7 7.4 %collective-permute-start.29 = (bf16[4,7,8,384]{3,2,1,0:T(8,128)(2,1)}, bf16[4,7,8,384]{3,2,1,0:T(8,128)(2,1)}, u32[]{:S(2)}, u32[]{:S(2)}) collective-permute-start(bf16[4,7,8,384]{3,2,1,0:T(8,128)(2,1)} %get-tuple-element.45), channel_id=1, source_target_pairs={{0,2},{1,3},{2,0},{3,1},{4,6},{5,7},{6,4},{7,5},{8,10},{9,11},{10,... | collective-permute-start | bytes 516104 | tf_op jit(solution)/shard_map/ppermute | solution.py:177
  190.3 15.5 %collective-permute-start.38 = (bf16[2,512,384]{2,1,0:T(8,128)(2,1)}, bf16[2,512,384]{2,1,0:T(8,128)(2,1)}, u32[]{:S(2)}, u32[]{:S(2)}) collective-permute-start(bf16[2,512,384]{2,1,0:T(8,128)(2,1)} %collective-permute-done.37.refs_1_), channel_id=1, source_target_pairs={{8,16},{16,24},{20,12},{12,4},{9,17},{17,25},{21,13},{13,5},{10,18... | collective-permute-start | bytes 2359304 | tf_op jit(solution)/shard_map/ppermute | solution.py:154
  191.9 15.6 %collective-permute-start.41 = (bf16[2,512,384]{2,1,0:T(8,128)(2,1)}, bf16[2,512,384]{2,1,0:T(8,128)(2,1)}, u32[]{:S(2)}, u32[]{:S(2)}) collective-permute-start(bf16[2,512,384]{2,1,0:T(8,128)(2,1)} %collective-permute-done.40.refs_5_), channel_id=1, source_target_pairs={{8,16},{16,24},{20,12},{12,4},{9,17},{17,25},{21,13},{13,5},{10,18... | collective-permute-start | bytes 2359304 | tf_op jit(solution)/shard_map/ppermute | solution.py:154
  194.1 6.7 %collective-permute-start.31 = (bf16[7,8,384]{2,1,0:T(8,128)(2,1)}, bf16[7,8,384]{2,1,0:T(8,128)(2,1)S(1)}, u32[]{:S(2)}, u32[]{:S(2)}) collective-permute-start(bf16[7,8,384]{2,1,0:T(8,128)(2,1)} %get-tuple-element.49), channel_id=1, source_target_pairs={{0,8},{4,12},{8,16},{12,20},{16,24},{20,28},{24,0},{28,4},{1,9},{5... | collective-permute-start | bytes 129032 | tf_op jit(solution)/shard_map/ppermute | solution.py:183
  198.7 5.0 %collective-permute-start.33 = (bf16[7,8,384]{2,1,0:T(8,128)(2,1)}, bf16[7,8,384]{2,1,0:T(8,128)(2,1)S(1)}, u32[]{:S(2)}, u32[]{:S(2)}) collective-permute-start(bf16[7,8,384]{2,1,0:T(8,128)(2,1)} %get-tuple-element.50), channel_id=1, source_target_pairs={{0,24},{4,28},{8,0},{12,4},{16,8},{20,12},{24,16},{28,20},{1,25},{... | collective-permute-start | bytes 129032 | tf_op jit(solution)/shard_map/ppermute | solution.py:183
  198.7 5.6 %collective-permute-start.32 = (bf16[7,8,384]{2,1,0:T(8,128)(2,1)S(1)}, bf16[7,8,384]{2,1,0:T(8,128)(2,1)S(1)}, u32[]{:S(2)}, u32[]{:S(2)}) collective-permute-start(bf16[7,8,384]{2,1,0:T(8,128)(2,1)S(1)} %get-tuple-element.51), channel_id=1, source_target_pairs={{0,16},{4,20},{8,24},{12,28},{16,0},{20,4},{24,8},{28,12},{1,17},{... | collective-permute-start | bytes 129032 | tf_op jit(solution)/shard_map/ppermute | solution.py:183
  200.7 3.0 %copy-start.9 = (bf16[7,8,384]{2,1,0:T(8,128)(2,1)}, bf16[7,8,384]{2,1,0:T(8,128)(2,1)S(1)}, u32[]{:S(2)}) copy-start(bf16[7,8,384]{2,1,0:T(8,128)(2,1)S(1)} %collective-permute-done.31) | copy-start | bytes 129028
  205.9 3.3 %collective-permute-start.39 = (bf16[2,512,384]{2,1,0:T(8,128)(2,1)}, bf16[2,512,384]{2,1,0:T(8,128)(2,1)}, u32[]{:S(2)}, u32[]{:S(2)}) collective-permute-start(bf16[2,512,384]{2,1,0:T(8,128)(2,1)} %collective-permute-done.38.refs_2_), channel_id=1, source_target_pairs={{16,24},{12,4},{17,25},{13,5},{18,26},{14,6},{19,27},{15,7}} | collective-permute-start | bytes 2359304 | tf_op jit(solution)/shard_map/ppermute | solution.py:154
  207.5 1.6 collective-permute-start.42
  218.6 32.7 %copy-start.5 = (bf16[56,32,384]{2,1,0:T(8,128)(2,1)S(1)}, bf16[56,32,384]{2,1,0:T(8,128)(2,1)}, u32[]{:S(2)}) copy-start(bf16[56,32,384]{2,1,0:T(8,128)(2,1)} %shard_map.82) | copy-start | bytes 4128772
  219.9 31.4 %collective-permute-start.43 = (bf16[4,7,4,8,384]{4,3,2,1,0:T(8,128)(2,1)S(1)}, bf16[4,7,4,8,384]{4,3,2,1,0:T(8,128)(2,1)S(1)}, u32[]{:S(2)}, u32[]{:S(2)}) collective-permute-start(bf16[4,7,4,8,384]{4,3,2,1,0:T(8,128)(2,1)S(1)} %dynamic-slice_bitcast_fusion), channel_id=1, source_target_pairs={{0,4},{4,0},{8,12},{12,8},{16,20},{20,16},{24,28},{28,24},{1,5},{5... | collective-permute-start | bytes 2064392 | tf_op jit(solution)/shard_map/ppermute | solution.py:172
  245.1 4.2 %collective-permute-start.34 = (bf16[7,8,384]{2,1,0:T(8,128)(2,1)S(1)}, bf16[7,8,384]{2,1,0:T(8,128)(2,1)S(1)}, u32[]{:S(2)}, u32[]{:S(2)}) collective-permute-start(bf16[7,8,384]{2,1,0:T(8,128)(2,1)S(1)} %get-tuple-element.37), channel_id=1, source_target_pairs={{0,1},{1,0},{2,3},{3,2},{4,5},{5,4},{6,7},{7,6},{8,9},{9,8},{10,11... | collective-permute-start | bytes 129032 | tf_op jit(solution)/shard_map/ppermute | solution.py:190
  246.7 8.5 %collective-permute-start.36 = (bf16[7,8,384]{2,1,0:T(8,128)(2,1)S(1)}, bf16[7,8,384]{2,1,0:T(8,128)(2,1)S(1)}, u32[]{:S(2)}, u32[]{:S(2)}) collective-permute-start(bf16[7,8,384]{2,1,0:T(8,128)(2,1)S(1)} %get-tuple-element.37), channel_id=1, source_target_pairs={{0,3},{1,2},{2,1},{3,0},{4,7},{5,6},{6,5},{7,4},{8,11},{9,10},{10,... | collective-permute-start | bytes 129032 | tf_op jit(solution)/shard_map/ppermute | solution.py:190
  247.3 4.0 %collective-permute-start.35 = (bf16[7,8,384]{2,1,0:T(8,128)(2,1)S(1)}, bf16[7,8,384]{2,1,0:T(8,128)(2,1)S(1)}, u32[]{:S(2)}, u32[]{:S(2)}) collective-permute-start(bf16[7,8,384]{2,1,0:T(8,128)(2,1)S(1)} %get-tuple-element.37), channel_id=1, source_target_pairs={{0,2},{1,3},{2,0},{3,1},{4,6},{5,7},{6,4},{7,5},{8,10},{9,11},{10,... | collective-permute-start | bytes 129032 | tf_op jit(solution)/shard_map/ppermute | solution.py:190
  251.6 7.2 %collective-permute-start.44 = (bf16[4,7,8,384]{3,2,1,0:T(8,128)(2,1)S(1)}, bf16[4,7,8,384]{3,2,1,0:T(8,128)(2,1)S(1)}, u32[]{:S(2)}, u32[]{:S(2)}) collective-permute-start(bf16[4,7,8,384]{3,2,1,0:T(8,128)(2,1)S(1)} %get-tuple-element.40), channel_id=1, source_target_pairs={{0,1},{1,0},{2,3},{3,2},{4,5},{5,4},{6,7},{7,6},{8,9},{9,8},{10,11... | collective-permute-start | bytes 516104 | tf_op jit(solution)/shard_map/ppermute | solution.py:177
  253.1 8.1 %collective-permute-start.46 = (bf16[4,7,8,384]{3,2,1,0:T(8,128)(2,1)S(1)}, bf16[4,7,8,384]{3,2,1,0:T(8,128)(2,1)S(1)}, u32[]{:S(2)}, u32[]{:S(2)}) collective-permute-start(bf16[4,7,8,384]{3,2,1,0:T(8,128)(2,1)S(1)} %get-tuple-element.41), channel_id=1, source_target_pairs={{0,3},{1,2},{2,1},{3,0},{4,7},{5,6},{6,5},{7,4},{8,11},{9,10},{10,... | collective-permute-start | bytes 516104 | tf_op jit(solution)/shard_map/ppermute | solution.py:177
  254.6 8.0 %collective-permute-start.45 = (bf16[4,7,8,384]{3,2,1,0:T(8,128)(2,1)S(1)}, bf16[4,7,8,384]{3,2,1,0:T(8,128)(2,1)S(1)}, u32[]{:S(2)}, u32[]{:S(2)}) collective-permute-start(bf16[4,7,8,384]{3,2,1,0:T(8,128)(2,1)S(1)} %get-tuple-element.42), channel_id=1, source_target_pairs={{0,2},{1,3},{2,0},{3,1},{4,6},{5,7},{6,4},{7,5},{8,10},{9,11},{10,... | collective-permute-start | bytes 516104 | tf_op jit(solution)/shard_map/ppermute | solution.py:177
  262.8 11.8 %collective-permute-start.47 = (bf16[7,8,384]{2,1,0:T(8,128)(2,1)S(1)}, bf16[7,8,384]{2,1,0:T(8,128)(2,1)S(1)}, u32[]{:S(2)}, u32[]{:S(2)}) collective-permute-start(bf16[7,8,384]{2,1,0:T(8,128)(2,1)S(1)} %get-tuple-element.46), channel_id=1, source_target_pairs={{0,8},{4,12},{8,16},{12,20},{16,24},{20,28},{24,0},{28,4},{1,9},{5... | collective-permute-start | bytes 129032 | tf_op jit(solution)/shard_map/ppermute | solution.py:183
  262.8 11.7 %collective-permute-start.49 = (bf16[7,8,384]{2,1,0:T(8,128)(2,1)S(1)}, bf16[7,8,384]{2,1,0:T(8,128)(2,1)S(1)}, u32[]{:S(2)}, u32[]{:S(2)}) collective-permute-start(bf16[7,8,384]{2,1,0:T(8,128)(2,1)S(1)} %get-tuple-element.47), channel_id=1, source_target_pairs={{0,24},{4,28},{8,0},{12,4},{16,8},{20,12},{24,16},{28,20},{1,25},{... | collective-permute-start | bytes 129032 | tf_op jit(solution)/shard_map/ppermute | solution.py:183
  272.6 4.9 %collective-permute-start.48 = (bf16[7,8,384]{2,1,0:T(8,128)(2,1)S(1)}, bf16[7,8,384]{2,1,0:T(8,128)(2,1)S(1)}, u32[]{:S(2)}, u32[]{:S(2)}) collective-permute-start(bf16[7,8,384]{2,1,0:T(8,128)(2,1)S(1)} %get-tuple-element.48), channel_id=1, source_target_pairs={{0,16},{4,20},{8,24},{12,28},{16,0},{20,4},{24,8},{28,12},{1,17},{... | collective-permute-start | bytes 129032 | tf_op jit(solution)/shard_map/ppermute | solution.py:183
  277.6 7.9 %copy-start.7 = (f32[224,768]{1,0:T(8,128)S(1)}, f32[224,768]{1,0:T(8,128)}, u32[]{:S(2)}) copy-start(f32[224,768]{1,0:T(8,128)} %param.9) | copy-start | bytes 2064388
  277.6 4.9 %collective-permute-start.50 = (bf16[7,8,384]{2,1,0:T(8,128)(2,1)S(1)}, bf16[7,8,384]{2,1,0:T(8,128)(2,1)S(1)}, u32[]{:S(2)}, u32[]{:S(2)}) collective-permute-start(bf16[7,8,384]{2,1,0:T(8,128)(2,1)S(1)} %get-tuple-element.39), channel_id=1, source_target_pairs={{0,1},{1,0},{2,3},{3,2},{4,5},{5,4},{6,7},{7,6},{8,9},{9,8},{10,11... | collective-permute-start | bytes 129032 | tf_op jit(solution)/shard_map/ppermute | solution.py:190
  279.5 4.0 %collective-permute-start.51 = (bf16[7,8,384]{2,1,0:T(8,128)(2,1)S(1)}, bf16[7,8,384]{2,1,0:T(8,128)(2,1)S(1)}, u32[]{:S(2)}, u32[]{:S(2)}) collective-permute-start(bf16[7,8,384]{2,1,0:T(8,128)(2,1)S(1)} %get-tuple-element.39), channel_id=1, source_target_pairs={{0,2},{1,3},{2,0},{3,1},{4,6},{5,7},{6,4},{7,5},{8,10},{9,11},{10,... | collective-permute-start | bytes 129032 | tf_op jit(solution)/shard_map/ppermute | solution.py:190
  280.5 4.9 %collective-permute-start.52 = (bf16[7,8,384]{2,1,0:T(8,128)(2,1)S(1)}, bf16[7,8,384]{2,1,0:T(8,128)(2,1)S(1)}, u32[]{:S(2)}, u32[]{:S(2)}) collective-permute-start(bf16[7,8,384]{2,1,0:T(8,128)(2,1)S(1)} %get-tuple-element.39), channel_id=1, source_target_pairs={{0,3},{1,2},{2,1},{3,0},{4,7},{5,6},{6,5},{7,4},{8,11},{9,10},{10,... | collective-permute-start | bytes 129032 | tf_op jit(solution)/shard_map/ppermute | solution.py:190
  (3 other events, 1.9 us)
